TPU v7x, 32 devices: a whole 2x2x4 slice. The times are simulated.
32 devices in a mesh: dp: 4 (over y, x), tensor: 8 (over z, core).
Axes of the slice: x: 2, y: 2, z: 4, core: 2. Of those that a mesh axis runs over, the one named last changes fastest.
Arguments:
- hidden: bfloat16 [16384, 2048], P(('dp', 'tensor')), may hold values from -160 to 160
- gain: float32 [2048], replicated, may hold values from 0.5 to 1.5
- bias: float32 [2048], replicated, may hold values from -3 to 3
- embedding: bfloat16 [49152, 2048], P('tensor'), may hold values from -8 to 8
- targets: int32 [16384], P('dp'), may hold values from 0 to 49151
- lengths: int32 [16], replicated, may hold values from 1 to 1024, 10240 in all
- owner: int32 [16], replicated, may hold values from 0 to 15, each once
Outputs:
- log_prob: float32 [16384], P(('dp', 'tensor'))
- entropy: float32 [16384], P(('dp', 'tensor'))
Inputs may be any that keep to these rules, and one draw needn't show every extreme that they name: `lengths`: each sequence's length is at most 1024, one is exactly 1024, and they sum to 10240. `owner`: a permutation of the sequences.
All inputs are finite; a program needn't handle non-finite values.
Results may differ from a plain program's by a relative error of at most 0.0036.
Values may be sent and summed in bfloat16 or wider, within the bound.
No kernel may reach another device: no remote copies, remote signals or barrier semaphores. Data moves between devices by JAX's collectives and lax.ppermute only.
A program may use at most 192 MiB of HBM per device.

v0:
```python
import jax
import jax.numpy as jnp
from jax import lax
from jax.sharding import PartitionSpec as P

SLOT = 1024
SEQ_GROUP = 4


EPS = 1e-05


def layer_norm(states, gain, bias):
    values = states.astype(jnp.float32)
    center = values - jnp.mean(values, axis=-1, keepdims=True)
    spread = jnp.mean(center * center, axis=-1, keepdims=True)
    return (center * lax.rsqrt(spread + EPS) * gain + bias).astype(jnp.bfloat16)


def shards(hidden, gain, bias, embedding, targets, lengths, owner):
    rows = hidden.shape[0]
    n_dp = lax.axis_size("dp")
    vocab_rows = embedding.shape[0]
    tp_index = lax.axis_index("tensor")
    dp_index = lax.axis_index("dp")
    voc_start = tp_index * vocab_rows
    columns = jnp.arange(vocab_rows, dtype=jnp.int32)
    logits = lax.dot_general(
        lax.all_gather(layer_norm(hidden, gain, bias), "tensor", axis=0, tiled=True),
        embedding,
        (((1,), (1,)), ((), ())),
        preferred_element_type=jnp.float32,
    )
    wanted = targets - voc_start
    picked = jnp.sum(jnp.where(columns[None, :] == wanted[:, None], logits, 0.0), axis=1)
    top = jnp.max(logits, axis=1)
    weights = jnp.exp(logits - top[:, None])
    total = jnp.sum(weights, axis=1)
    moment = jnp.sum(weights * logits, axis=1)
    gathered = jnp.stack([top, total, moment, picked], axis=0)
    local_top = gathered[0]
    top = lax.pmax(local_top, "tensor")
    factor = jnp.exp(local_top - top)
    total, moment, picked = lax.psum(
        (gathered[1] * factor, gathered[2] * factor, gathered[3]), "tensor"
    )
    logz = top + jnp.log(total)
    token_lp = (picked - logz).reshape(SEQ_GROUP, SLOT)
    token_ent = (logz - moment / total).reshape(SEQ_GROUP, SLOT)
    group_lengths = lax.dynamic_slice_in_dim(lengths, dp_index * SEQ_GROUP, SEQ_GROUP)
    valid = jnp.arange(SLOT, dtype=jnp.int32)[None, :] < group_lengths[:, None]
    results = jnp.stack([jnp.where(valid, token_lp, 0.0), jnp.where(valid, token_ent, 0.0)], axis=0)
    offset = tp_index * rows % SLOT
    slot_here = tp_index * rows // SLOT
    mine = lax.dynamic_slice_in_dim(results, offset, rows, 2)
    group_owner = lax.dynamic_slice_in_dim(owner, dp_index * SEQ_GROUP, SEQ_GROUP)
    wanted_slot = jnp.arange(n_dp, dtype=jnp.int32) * SEQ_GROUP + slot_here
    select = (group_owner[None, :] == wanted_slot[:, None]).astype(jnp.float32)
    outgoing = jnp.einsum("hs,csr->hcr", select, mine, precision=lax.Precision.HIGHEST)
    incoming = lax.all_to_all(outgoing, "dp", split_axis=0, concat_axis=0, tiled=True)
    combined = jnp.sum(incoming, axis=0)
    return (combined[0], combined[1])


def solution(mesh):
    in_specs = (P(("dp", "tensor"), None), P(), P(), P("tensor", None), P("dp"), P(), P())
    out_specs = (P(("dp", "tensor")), P(("dp", "tensor")))
    return jax.shard_map(shards, mesh=mesh, in_specs=in_specs, out_specs=out_specs, check_vma=False)
```

profile of v0, /device:TPU:0, one launch (start us, length us, event | category | flops | bytes accessed | tf_op | source)
XLA Modules:
  0.0 391.4 jit_solution(5191159960536429483)
XLA Ops:
  7.2 0.0 all-gather.2.cloned.1.call-start
  7.2 1.9 convert_reduce_fusion
  9.2 2.3 fusion.3
  11.4 3.8 fusion.6
  15.2 0.0 all-gather.2.cloned.1.call-update
  15.3 1.2 dynamic_slice.10
  16.5 1.2 dynamic_slice.9
  17.8 0.6 multiply_add_fusion
  18.4 1.3 broadcast_subtract_fusion
  19.7 149.6 %all-gather.2.cloned.1.call-done = bf16[4096,2048]{1,0:T(8,128)(2,1)} async-done(((bf16[512,2048]{1,0:T(8,128)(2,1)}), bf16[4096,2048]{1,0:T(8,128)(2,1)}) %all-gather.2.cloned.1.call-update) | async-done | bytes 16777232 | tf_op jit(solution)/shard_map/all_gather | solution.py:29
  169.2 115.2 %fusion.22 = (f32[4096]{0:T(1024)S(1)}, f32[4096,6144]{1,0:T(8,128)}) fusion(bf16[4096,2048]{1,0:T(8,128)(2,1)} %all-gather.2.cloned.1.call-done, bf16[6144,2048]{1,0:T(8,128)(2,1)} %param.10), kind=kOutput, calls=%fused_computation.37 | convolution fusion | flops 103104380928 | bytes 142622720 | tf_op jit(solution)/shard_map/dot_general | solution.py:28
  284.5 26.0 %pmax.7 = f32[4096]{0:T(1024)S(1)} all-reduce(f32[4096]{0:T(1024)S(1)} %get-tuple-element.16), channel_id=1, replica_groups=mesh['dp'=4,'tensor'=8] {'tensor'}, use_global_device_ids=true, to_apply=%region_5.6 | all-reduce | flops 4096 | bytes 32768 | tf_op jit(solution)/shard_map/pmax | solution.py:42
  310.5 0.0 copy-done
  310.5 0.0 copy-start.1
  310.5 0.0 copy-start.2
  310.5 38.4 %multiply_reduce_fusion = (f32[4096]{0:T(1024)S(1)}, f32[4096]{0:T(1024)S(1)}, f32[4096]{0:T(1024)S(1)}) fusion(f32[4096,6144]{1,0:T(8,128)} %get-tuple-element.17, f32[4096]{0:T(1024)S(1)} %get-tuple-element.16, s32[4096]{0:T(1024)S(1)} %copy-done), kind=kLoop, calls=%fused_computation | loop fusion | flops 176148480 | bytes 100745216 | tf_op jit(solution)/shard_map/reduce_sum | solution.py:39
  348.9 26.4 %all-reduce = (f32[4096]{0:T(1024)S(1)}, f32[4096]{0:T(1024)S(1)}, f32[4096]{0:T(1024)S(1)}) all-reduce(f32[4096]{0:T(1024)S(1)} %get-tuple-element.4, f32[4096]{0:T(1024)S(1)} %get-tuple-element.11, f32[4096]{0:T(1024)S(1)} %get-tuple-element.10), channel_id=1, replica_groups=mesh['dp'=4,'tensor'=8] {'tensor'}, use_global_device_ids=true, to_apply=%region_3.4 | all-reduce | flops 12288 | bytes 98304 | tf_op jit(solution)/shard_map/psum | solution.py:44
  375.3 0.0 copy-done.1
  375.3 0.1 fusion.10
  375.4 0.0 copy-done.2
  375.4 0.0 copy-done.3
  375.4 0.2 fusion.8
  375.6 8.3 %all_to_all.5 = f32[4,2,512]{2,1,0:T(2,128)S(1)} all-to-all(f32[4,2,512]{2,1,0:T(2,128)S(1)} %copy.9), channel_id=1, replica_groups=mesh['dp'=4,'tensor'=8] {'dp'}, dimensions={0} | all-to-all | bytes 32768 | tf_op jit(solution)/shard_map/all_to_all | solution.py:60
  383.9 0.6 fusion.21
  (10 shorter events, 0.1 us)
Async XLA Ops:
  7.2 162.1 %all-gather.2.cloned.1.call-start = ((), (), s32[]{:S(2)}) async-start(), calls=%async_computation.1 | async-start | bytes 18874368 | tf_op jit(solution)/shard_map/all_gather | solution.py:29
  169.2 141.3 %copy-start = (s32[4096]{0:T(1024)S(1)}, s32[4096]{0:T(1024)}, u32[]{:S(2)}) copy-start(s32[4096]{0:T(1024)} %broadcast_subtract_fusion) | copy-start | bytes 49156
  310.5 64.8 %copy-start.1 = (s32[4]{0:T(128)S(1)}, s32[4]{0:T(128)}, u32[]{:S(2)}) copy-start(s32[4]{0:T(128)} %dynamic_slice.10) | copy-start | bytes 52
  310.5 64.9 %copy-start.2 = (s32[4]{0:T(128)S(1)}, s32[4]{0:T(128)}, u32[]{:S(2)}) copy-start(s32[4]{0:T(128)} %dynamic_slice.9) | copy-start | bytes 52
  310.5 64.9 %copy-start.3 = (s32[4]{0:T(128)S(1)}, s32[4]{0:T(128)}, u32[]{:S(2)}) copy-start(s32[4]{0:T(128)} %multiply_add_fusion) | copy-start | bytes 52
Sparse Core Ops, SparseCore 0:
  15.4 153.7 all-gather.1
where the time goes:
time: 392 us; the launch traced here: 391 us
  waiting for transfers between devices  150 us (38%)
  matrix products  115 us (29%)
  blocking collectives  60.7 us (15%)
  other arithmetic  48.4 us (12%)
  between operations  14.1 us (4%)
    all_gather x1, waiting for transfers between devices, shards(): lax.all_gather(layer_norm(hidden, gain, bias), 'tensor', axis=0, tiled=True)  150 us
    dot_general x1, matrix products, shards(): lax.dot_general(lax.all_gather(layer_norm(hidden, gain, bias), 'tensor',...  115 us
    reduce_sum x1, other arithmetic, shards(): moment = jnp.sum(weights * logits, axis=1)  38.4 us
    psum x1, blocking collectives, shards(): lax.psum((gathered[1] * factor, gathered[2] * factor, gathered[3]), 'tens...  26.4 us
    pmax x1, blocking collectives, shards(): top = lax.pmax(local_top, 'tensor')  26 us
    all_to_all x1, blocking collectives, shards(): lax.all_to_all(outgoing, 'dp', split_axis=0, concat_axis=0, tiled=True)  8.29 us
  transfers between devices with their start and end apart: 1, of which 1 were waited for; matrix products, arithmetic and copies ran while one was open for 1% of the time, Pallas kernels for 0%

commit v1 on v0

v1 whole, which is shorter than its diff:
```python
import functools
import math

import jax
import jax.numpy as jnp
from jax import lax
from jax.experimental import pallas as pl
from jax.experimental.pallas import tpu as pltpu
from jax.sharding import PartitionSpec as P

SLOT = 1024
BLOCK = 128
GROUP = 2 * BLOCK
EPS = 1e-05
LOG2E = 1.4426950408889634
LN2 = 0.6931471805599453
LOWEST = -1e30


def layer_norm(states, gain, bias):
    values = states.astype(jnp.float32)
    center = values - jnp.mean(values, axis=-1, keepdims=True)
    spread = jnp.mean(center * center, axis=-1, keepdims=True)
    return (center * lax.rsqrt(spread + EPS) * gain + bias).astype(jnp.bfloat16)


def score_kernel(chunk, blocks, sub, live_ref, start_ref, rows_ref, t_ref, e_ref, o_ref, x_ref, state, order, sems):
    step, steps = pl.program_id(0), pl.num_programs(0)
    tile = e_ref.shape[0]

    def copy(j, place):
        return pltpu.make_async_copy(
            rows_ref.at[pl.ds(j * BLOCK, BLOCK)], x_ref.at[pl.ds(pl.multiple_of(place * BLOCK, BLOCK), BLOCK)], sems.at[j]
        )

    @pl.when(step == 0)
    def _():
        state[:, 0] = jnp.full((blocks // 2, 8, GROUP), LOWEST, jnp.float32)
        state[:, 1:4] = jnp.zeros((blocks // 2, 3, 8, GROUP), jnp.float32)
        o_ref[...] = jnp.zeros_like(o_ref)
        count = jnp.int32(0)
        for j in range(blocks):
            alive = live_ref[chunk, j] > 0

            @pl.when(alive)
            def _():
                order[count] = j
                copy(j, count).start()

            count = count + alive.astype(jnp.int32)
        order[blocks] = count

        @pl.when(count < blocks)
        def _():
            order[count] = blocks

        place = jnp.int32(0)
        for j in range(blocks):
            alive = live_ref[chunk, j] > 0
            pl.when(alive)(copy(j, place).wait)
            place = place + alive.astype(jnp.int32)

    for g in range(blocks // 2):

        @pl.when(2 * g < order[blocks])
        def _():
            x = x_ref[g * GROUP : (g + 1) * GROUP, :]
            first, second = order[2 * g], order[2 * g + 1]
            wanted = jnp.concatenate([t_ref[first], t_ref[second]], axis=1)
            wanted = wanted - start_ref[0] - step * tile - lax.broadcasted_iota(jnp.int32, (8, GROUP), 0)
            top, total, moment, picked = (state[g, i] for i in range(4))
            for s in range(0, tile, sub):
                logits = lax.dot_general(
                    e_ref[s : s + sub, :], x, (((1,), (1,)), ((), ())), preferred_element_type=jnp.float32
                )
                logits = logits.reshape(sub // 8, 8, GROUP) * LOG2E
                index = lax.broadcasted_iota(jnp.int32, (sub // 8, 8, GROUP), 0) * 8 + s
                new = jnp.maximum(top, jnp.max(logits, axis=0))
                lower = top - new
                factor = jnp.exp2(lower)
                delta = logits - new[None]
                weights = jnp.exp2(delta)
                moment = factor * (moment + total * lower) + jnp.sum(weights * delta, axis=0)
                total = factor * total + jnp.sum(weights, axis=0)
                picked = picked + jnp.sum(jnp.where(wanted[None] == index, logits, 0.0), axis=0)
                top = new
            for i, value in enumerate((top, total, moment, picked)):
                state[g, i] = value

            @pl.when(step == steps - 1)
            def _():
                highest = jnp.max(top, axis=0, keepdims=True)
                lower = top - highest
                factor = jnp.exp2(lower)
                result = jnp.concatenate(
                    [
                        highest,
                        jnp.sum(total * factor, axis=0, keepdims=True),
                        jnp.sum((moment + total * lower) * factor, axis=0, keepdims=True),
                        jnp.sum(picked, axis=0, keepdims=True),
                    ],
                    axis=0,
                )
                o_ref[first, 0:4] = result[:, 0:BLOCK]
                o_ref[second, 0:4] = result[:, BLOCK:GROUP]


def score(chunk, rows, table, targets, live, start):
    blocks, (vocab, width) = rows.shape[0] // BLOCK, table.shape
    tile = math.gcd(vocab, 768)
    sub = math.gcd(tile, 256)
    hbm = lambda a: pltpu.with_memory_space_constraint(a, pltpu.HBM)
    return pl.pallas_call(
        functools.partial(score_kernel, chunk, blocks, sub),
        out_shape=jax.ShapeDtypeStruct((blocks + 1, 8, BLOCK), jnp.float32),
        grid_spec=pltpu.PrefetchScalarGridSpec(
            num_scalar_prefetch=2,
            grid=(vocab // tile,),
            in_specs=[
                pl.BlockSpec(memory_space=pl.ANY),
                pl.BlockSpec((blocks + 1, 1, BLOCK), lambda i, *_: (0, 0, 0)),
                pl.BlockSpec((tile, width), lambda i, *_: (i, 0)),
            ],
            out_specs=pl.BlockSpec((blocks + 1, 8, BLOCK), lambda i, *_: (0, 0, 0)),
            scratch_shapes=[
                pltpu.VMEM((blocks * BLOCK, width), jnp.bfloat16),
                pltpu.VMEM((blocks // 2, 4, 8, GROUP), jnp.float32),
                pltpu.SMEM((blocks + 1,), jnp.int32),
                pltpu.SemaphoreType.DMA((blocks,)),
            ],
        ),
        compiler_params=pltpu.CompilerParams(vmem_limit_bytes=40 * 2**20),
        cost_estimate=pl.CostEstimate(
            flops=blocks * BLOCK * vocab * width * 2,
            bytes_accessed=vocab * width * 2,
            transcendentals=blocks * BLOCK * vocab,
        ),
    )(live, start, hbm(rows), targets, hbm(table))


def column_stats(normed, table, targets, lengths, start):
    rows, n_tensor = normed.shape[0], lax.axis_size("tensor")
    each = min(rows, BLOCK)
    chunks, blocks = rows // each, n_tensor * each // BLOCK
    stride = max(rows, BLOCK)
    first = jnp.arange(chunks)[:, None] * BLOCK + jnp.arange(blocks)[None, :] * stride
    live = jnp.clip(lengths[first // SLOT] - first % SLOT, 0, BLOCK).astype(jnp.int32)
    targets = targets.reshape(blocks, chunks, 1, BLOCK)
    spare = jnp.full((1, 1, BLOCK), -1, jnp.int32)
    done = []
    for c in range(chunks):
        gathered = lax.all_gather(normed[c * each : (c + 1) * each], "tensor", axis=0, tiled=True)
        wanted = jnp.concatenate([targets[:, c], spare], axis=0)
        done.append(score(c, gathered, table, wanted, live, start)[:blocks, :4])
    return jnp.stack(done, axis=1).reshape(blocks * chunks, 4, BLOCK)


def shards(hidden, gain, bias, embedding, targets, lengths, owner):
    rows = hidden.shape[0]
    n_dp, n_tensor = lax.axis_size("dp"), lax.axis_size("tensor")
    tp_index, dp_index = lax.axis_index("tensor"), lax.axis_index("dp")
    group = lengths.shape[0] // n_dp
    start = (tp_index * embedding.shape[0]).astype(jnp.int32)[None]
    own_lengths = lax.dynamic_slice_in_dim(lengths, dp_index * group, group)
    stats = column_stats(layer_norm(hidden, gain, bias), embedding, targets, own_lengths, start)
    parts = SLOT // rows
    stats = stats.reshape(group, SLOT // BLOCK, 4, BLOCK).transpose(0, 2, 1, 3).reshape(group, 4, parts, rows)
    stats = stats.transpose(0, 2, 1, 3)
    came_from = jnp.argsort(owner).astype(jnp.int32)
    local = came_from.reshape(n_dp, group) - dp_index * group
    outgoing = jnp.zeros((n_dp, group, parts, 4, rows), jnp.float32)
    for s in range(group):
        outgoing = jnp.where((local == s)[:, :, None, None, None], stats[s][None, None], outgoing)
    incoming = lax.all_to_all(
        outgoing.reshape(n_dp * n_tensor, 4, rows), ("dp", "tensor"), split_axis=0, concat_axis=0, tiled=True
    )
    place = dp_index * group + tp_index // parts
    sequence = lax.dynamic_slice_in_dim(came_from, place, 1)[0]
    incoming = incoming.reshape(n_dp, n_tensor, 4, rows)
    mine = lax.dynamic_slice_in_dim(incoming, sequence // group, 1, 0)[0]
    top = jnp.max(mine[:, 0], axis=0)
    lower = mine[:, 0] - top[None]
    factor = jnp.exp2(lower)
    total = jnp.sum(mine[:, 1] * factor, axis=0)
    moment = jnp.sum((mine[:, 2] + mine[:, 1] * lower) * factor, axis=0)
    picked = jnp.sum(mine[:, 3], axis=0)
    log_total = jnp.log(total)
    token_lp = (picked - top) * LN2 - log_total
    token_ent = log_total - moment * LN2 / total
    length = lax.dynamic_slice_in_dim(lengths, sequence, 1)[0]
    valid = jnp.arange(rows, dtype=jnp.int32) + tp_index % parts * rows < length
    return jnp.where(valid, token_lp, 0.0), jnp.where(valid, token_ent, 0.0)


def solution(mesh):
    in_specs = (P(("dp", "tensor"), None), P(), P(), P("tensor", None), P("dp"), P(), P())
    out_specs = (P(("dp", "tensor")), P(("dp", "tensor")))
    return jax.shard_map(shards, mesh=mesh, in_specs=in_specs, out_specs=out_specs, check_vma=False)
```

time: 392 us -> 272 us (0.69)
  matrix products: 115 us -> 0 us
  Pallas kernels: 0 us -> 88.7 us
  blocking collectives: 60.7 us -> 0 us
  other arithmetic: 48.4 us -> 8.88 us
  starting transfers between devices: 0.04 us -> 13 us
  waiting for transfers between devices: 150 us -> 138 us
    dot_general x2 -> x0, matrix products: 115 us -> none  [the longest x1 115 us: shards(): lax.dot_general(lax.all_gather(layer_norm(hidden, gain, bias), 'tensor',...]
    pallas_call x0 -> x4, Pallas kernels: none -> 88.7 us  [score(): pl.pallas_call(functools.partial(score_kernel, chunk, blocks, sub), out_s...]
    reduce_sum x2 -> x1, other arithmetic: 38.4 us -> 0.03 us  [shards(): moment = jnp.sum((mine[:, 2] + mine[:, 1] * lower) * factor, axis=0)]
    psum x1 -> x0, blocking collectives: 26.4 us -> none  [shards(): lax.psum((gathered[1] * factor, gathered[2] * factor, gathered[3]), 'tens...]
    pmax x1 -> x0, blocking collectives: 26 us -> none  [shards(): top = lax.pmax(local_top, 'tensor')]
    all_gather x1 -> x4, waiting for transfers between devices: 150 us -> 131 us  [column_stats(): lax.all_gather(normed[c * each:(c + 1) * each], 'tensor', axis=0, tiled=T...]
    all_to_all x0 -> x1, starting transfers between devices: none -> 12.9 us  [shards(): lax.all_to_all(outgoing.reshape(n_dp * n_tensor, 4, rows), ('dp', 'tensor...]
    all_to_all x1 -> x0, blocking collectives: 8.29 us -> none  [shards(): lax.all_to_all(outgoing, 'dp', split_axis=0, concat_axis=0, tiled=True)]
  transfers between devices with their start and end apart: 1 -> 5, of which waited for: 1 -> 5; matrix products, arithmetic and copies ran while one was open for 1% -> 2% of each run, Pallas kernels for 0% -> 21%
where the time goes in v1:
time: 272 us; the launch traced here: 271 us
  waiting for transfers between devices  138 us (51%)
  Pallas kernels  88.7 us (33%)
  between operations  18 us (7%)
  starting transfers between devices  13 us (5%)
  other arithmetic  8.88 us (3%)
  local copies, waits for them, and re-layouts  4.94 us (2%)
    all_gather x4, waiting for transfers between devices, column_stats(): lax.all_gather(normed[c * each:(c + 1) * each], 'tensor', axis=0, tiled=T...  131 us
    pallas_call x4, Pallas kernels, score(): pl.pallas_call(functools.partial(score_kernel, chunk, blocks, sub), out_s...  88.7 us
    all_to_all x1, starting transfers between devices, shards(): lax.all_to_all(outgoing.reshape(n_dp * n_tensor, 4, rows), ('dp', 'tensor...  12.9 us
  transfers between devices with their start and end apart: 5, of which 5 were waited for; matrix products, arithmetic and copies ran while one was open for 2% of the time, Pallas kernels for 21%

profile of v1, /device:TPU:0, one launch (start us, length us, event | category | flops | bytes accessed | tf_op | source)
XLA Modules:
  0.0 271.3 jit_solution(5311238475181417951)
XLA Ops:
  7.2 2.1 convert_reduce_fusion
  9.3 2.3 fusion.2
  11.6 0.8 fusion.5
  12.5 1.4 fusion.18
  14.0 0.7 all-gather.9.cloned.1.call-update
  14.7 0.7 all-gather.7.cloned.1.call-update
  15.5 0.5 all-gather.5.cloned.1.call-update
  16.3 0.7 gather_fusion
  17.2 1.2 sort.17
  18.9 0.1 broadcast_in_dim.116
  19.6 44.3 %all-gather.11.cloned.1.call-done.rows_ref = bf16[1024,2048]{1,0:T(8,128)(2,1)} async-done(((bf16[128,2048]{1,0:T(8,128)(2,1)}), bf16[1024,2048]{1,0:T(8,128)(2,1)}) %all-gather.11.cloned.1.call-update) | async-done | bytes 4194320 | tf_op jit(solution)/shard_map/all_gather | solution.py:152
  63.9 16.4 %shard_map.89 = f32[9,8,128]{2,1,0:T(8,128)S(1)} custom-call(s32[4,8]{1,0:T(4,128)S(1)} %fusion.14.live_ref, s32[1]{0:T(128)} %bitcast.2.start_ref, bf16[1024,2048]{1,0:T(8,128)(2,1)} %all-gather.11.cloned.1.call-done.rows_ref, s32[9,1,128]{2,1,0:T(1,128)S(1)} %concatenate.15.t_ref, bf16[6144,2048]{1,0:T(8,128)(2,1)} %e_ref.7), custom_call_target="tpu_custom_call" | custom-call | flops 25769803776 | bytes 25165824 | tf_op jit(solution)/shard_map/pallas_call | solution.py:113
  80.3 31.1 %all-gather.9.cloned.1.call-done.rows_ref = bf16[1024,2048]{1,0:T(8,128)(2,1)} async-done(((bf16[128,2048]{1,0:T(8,128)(2,1)}), bf16[1024,2048]{1,0:T(8,128)(2,1)}) %all-gather.9.cloned.1.call-update) | async-done | bytes 4194320 | tf_op jit(solution)/shard_map/all_gather | solution.py:152
  111.4 16.4 %shard_map.88 = f32[9,8,128]{2,1,0:T(8,128)S(1)} custom-call(s32[4,8]{1,0:T(4,128)S(1)} %fusion.14.live_ref, s32[1]{0:T(128)} %bitcast.2.start_ref, bf16[1024,2048]{1,0:T(8,128)(2,1)} %all-gather.9.cloned.1.call-done.rows_ref, s32[9,1,128]{2,1,0:T(1,128)S(1)} %concatenate.14.t_ref, bf16[6144,2048]{1,0:T(8,128)(2,1)} %e_ref.7), custom_call_target="tpu_custom_call" | custom-call | flops 25769803776 | bytes 25165824 | tf_op jit(solution)/shard_map/pallas_call | solution.py:113
  127.8 31.2 %all-gather.7.cloned.1.call-done.rows_ref = bf16[1024,2048]{1,0:T(8,128)(2,1)} async-done(((bf16[128,2048]{1,0:T(8,128)(2,1)}), bf16[1024,2048]{1,0:T(8,128)(2,1)}) %all-gather.7.cloned.1.call-update) | async-done | bytes 4194320 | tf_op jit(solution)/shard_map/all_gather | solution.py:152
  159.0 23.3 %shard_map.87 = f32[9,8,128]{2,1,0:T(8,128)S(1)} custom-call(s32[4,8]{1,0:T(4,128)S(1)} %fusion.14.live_ref, s32[1]{0:T(128)} %bitcast.2.start_ref, bf16[1024,2048]{1,0:T(8,128)(2,1)} %all-gather.7.cloned.1.call-done.rows_ref, s32[9,1,128]{2,1,0:T(1,128)S(1)} %concatenate.13.t_ref, bf16[6144,2048]{1,0:T(8,128)(2,1)} %e_ref.7), custom_call_target="tpu_custom_call" | custom-call | flops 25769803776 | bytes 25165824 | tf_op jit(solution)/shard_map/pallas_call | solution.py:113
  182.3 24.0 %all-gather.5.cloned.1.call-done.rows_ref = bf16[1024,2048]{1,0:T(8,128)(2,1)} async-done(((bf16[128,2048]{1,0:T(8,128)(2,1)}), bf16[1024,2048]{1,0:T(8,128)(2,1)}) %all-gather.5.cloned.1.call-update) | async-done | bytes 4194320 | tf_op jit(solution)/shard_map/all_gather | solution.py:152
  206.3 32.6 %shard_map.86 = f32[9,8,128]{2,1,0:T(8,128)S(1)} custom-call(s32[4,8]{1,0:T(4,128)S(1)} %fusion.14.live_ref, s32[1]{0:T(128)} %bitcast.2.start_ref, bf16[1024,2048]{1,0:T(8,128)(2,1)} %all-gather.5.cloned.1.call-done.rows_ref, s32[9,1,128]{2,1,0:T(1,128)S(1)} %concatenate.12.t_ref, bf16[6144,2048]{1,0:T(8,128)(2,1)} %e_ref.7), custom_call_target="tpu_custom_call" | custom-call | flops 25769803776 | bytes 25165824 | tf_op jit(solution)/shard_map/pallas_call | solution.py:113
  239.1 0.9 fusion.8
  240.0 12.9 %all-to-all-start = ((f32[32,4,512]{2,1,0:T(4,128)}), f32[32,4,512]{2,1,0:T(4,128)S(1)}, u32[]{:S(2)}, u32[]{:S(2)}) async-start(f32[32,4,512]{2,1,0:T(4,128)} %fusion.8), calls=%async_computation | async-start | bytes 524288 | tf_op jit(solution)/shard_map/all_to_all | solution.py:174
  252.9 0.6 dynamic_slice.12
  257.4 0.7 dynamic_slice.13
  258.1 5.2 %all-to-all-done = f32[32,4,512]{2,1,0:T(4,128)S(1)} async-done(((f32[32,4,512]{2,1,0:T(4,128)}), f32[32,4,512]{2,1,0:T(4,128)S(1)}, u32[]{:S(2)}, u32[]{:S(2)}) %all-to-all-start) | async-done | bytes 262176 | tf_op jit(solution)/shard_map/all_to_all | solution.py:174
  263.4 1.3 subtract_select_fusion
  (62 shorter events, 2.0 us)
Async XLA Ops:
  7.2 4.5 %copy-start = (bf16[512,2048]{1,0:T(8,128)(2,1)S(1)}, bf16[512,2048]{1,0:T(8,128)(2,1)}, u32[]{:S(2)}) copy-start(bf16[512,2048]{1,0:T(8,128)(2,1)} %param.7) | copy-start | bytes 6291460
  7.2 4.4 %copy-start.2 = (f32[2048]{0:T(1024)S(1)}, f32[2048]{0:T(1024)}, u32[]{:S(2)}) copy-start(f32[2048]{0:T(1024)} %param.9) | copy-start | bytes 24580
  7.2 4.4 %copy-start.3 = (f32[2048]{0:T(1024)S(1)}, f32[2048]{0:T(1024)}, u32[]{:S(2)}) copy-start(f32[2048]{0:T(1024)} %param.8) | copy-start | bytes 24580
  7.2 56.7 %all-gather.11.cloned.1.call-start = ((), (), s32[]{:S(2)}) async-start(), calls=%async_computation.4 | async-start | bytes 4718592 | tf_op jit(solution)/shard_map/all_gather | solution.py:152
  12.5 3.7 %copy-start.5 = (s32[16]{0:T(128)S(1)}, s32[16]{0:T(128)}, u32[]{:S(2)}) copy-start(s32[16]{0:T(128)} %param.12) | copy-start | bytes 196
  12.5 4.6 %copy-start.1 = (s32[4096]{0:T(1024)S(1)}, s32[4096]{0:T(1024)}, u32[]{:S(2)}) copy-start(s32[4096]{0:T(1024)} %param.11) | copy-start | bytes 49156
  12.5 4.7 %copy-start.4 = (s32[16]{0:T(128)S(1)}, s32[16]{0:T(128)}, u32[]{:S(2)}) copy-start(s32[16]{0:T(128)} %param.13) | copy-start | bytes 196
  13.9 97.5 %all-gather.9.cloned.1.call-start = ((), (), s32[]{:S(2)}) async-start(), calls=%async_computation.3 | async-start | bytes 4718592 | tf_op jit(solution)/shard_map/all_gather | solution.py:152
  14.7 144.3 %all-gather.7.cloned.1.call-start = ((), (), s32[]{:S(2)}) async-start(), calls=%async_computation.2 | async-start | bytes 4718592 | tf_op jit(solution)/shard_map/all_gather | solution.py:152
  15.4 190.9 %all-gather.5.cloned.1.call-start = ((), (), s32[]{:S(2)}) async-start(), calls=%async_computation.1 | async-start | bytes 4718592 | tf_op jit(solution)/shard_map/all_gather | solution.py:152
  240.0 23.3 %all-to-all-start = ((f32[32,4,512]{2,1,0:T(4,128)}), f32[32,4,512]{2,1,0:T(4,128)S(1)}, u32[]{:S(2)}, u32[]{:S(2)}) async-start(f32[32,4,512]{2,1,0:T(4,128)} %fusion.8), calls=%async_computation | async-start | bytes 524288 | tf_op jit(solution)/shard_map/all_to_all | solution.py:174
Sparse Core Ops, SparseCore 0:
  14.0 49.8 all-gather.10
  65.5 45.8 all-gather.8
  113.0 45.9 all-gather.6
  160.4 45.7 all-gather.4

commit v2 on v0

v2 whole, which is shorter than its diff:
```python
import functools
import math

import jax
import jax.numpy as jnp
from jax import lax
from jax.experimental import pallas as pl
from jax.experimental.pallas import tpu as pltpu
from jax.sharding import PartitionSpec as P

SLOT = 1024
BLOCK = 128
WIDE = 4
EPS = 1e-05
LOG2E = 1.4426950408889634
LN2 = 0.6931471805599453
LOWEST = -1e30


def layer_norm(states, gain, bias):
    values = states.astype(jnp.float32)
    center = values - jnp.mean(values, axis=-1, keepdims=True)
    spread = jnp.mean(center * center, axis=-1, keepdims=True)
    return (center * lax.rsqrt(spread + EPS) * gain + bias).astype(jnp.bfloat16)


def score_kernel(call, sources, arrivals, shares, per, capacity, sub, lengths_ref, *refs):
    count = sum(arrival <= call for arrival in arrivals)
    rows_refs, (t_ref, e_ref), refs = refs[:count], refs[count : count + 2], refs[count + 2 :]
    stats_ref, (o_ref, x_ref, state, order, sems) = (None if call == 0 else refs[0]), refs[-5:]
    step, steps = pl.program_id(0), pl.num_programs(0)
    tile = e_ref.shape[0]
    spare = o_ref.shape[0] - 1
    slots = SLOT // BLOCK
    n_dp, n_tensor = lax.axis_size("dp"), lax.axis_size("tensor")
    group_size = lengths_ref.shape[0] // n_dp
    before = lax.axis_index("dp") * group_size
    start = lax.axis_index("tensor") * e_ref.shape[0] * steps
    chip, core = lax.axis_index("tensor") // 2, lax.axis_index("tensor") % 2

    def copy(ref, j, place):
        return pltpu.make_async_copy(
            ref.at[pl.ds(j * BLOCK, BLOCK)],
            x_ref.at[pl.ds(pl.multiple_of(place * BLOCK, BLOCK), BLOCK)],
            sems.at[place],
        )

    @pl.when(step == 0)
    def _():
        o_ref[...] = jnp.zeros_like(o_ref) if stats_ref is None else stats_ref[...]
        total = jnp.int32(0)
        for s in range(group_size):
            total = total + (lengths_ref[before + s] + BLOCK - 1) // BLOCK
        limits = [(total * share + 31) // 32 for share in shares]
        used, rank = jnp.int32(0), jnp.int32(0)
        for i in range(count):
            if sources is None:
                first, inside = jnp.int32(0), True
            else:
                away, crossed = sources[i]
                layer = chip + away * (2 * core - 1)
                half = core if not crossed else 1 - core
                inside = (layer >= 0) & (layer < n_tensor // 2)
                first = jnp.clip(layer, 0, n_tensor // 2 - 1) * slots + half * per
            for j in range(per):
                place = first + j
                live = inside & (lengths_ref[before + place // slots] > place % slots * BLOCK)
                mine = live
                if call > 0 and arrivals[i] < call:
                    mine = mine & (rank >= limits[call - 1])
                if call < len(shares):
                    mine = mine & (rank < limits[call])

                @pl.when(mine)
                def _():
                    order[used] = place
                    copy(rows_refs[i], j, used).start()

                used = used + mine.astype(jnp.int32)
                rank = rank + live.astype(jnp.int32)
        order[capacity + WIDE] = used
        for j in range(WIDE):
            order[used + j] = spare

    used = order[capacity + WIDE]

    def group(g, width):
        lanes = width * BLOCK
        begin = pl.multiple_of(g * (WIDE * BLOCK), WIDE * BLOCK)

        @pl.when(step == 0)
        def _():
            state[g, 0, :, 0:lanes] = jnp.full((8, lanes), LOWEST, jnp.float32)
            state[g, 1:4, :, 0:lanes] = jnp.zeros((3, 8, lanes), jnp.float32)
            for j in range(width):
                pl.when(g * WIDE + j < used)(copy(rows_refs[0], 0, g * WIDE + j).wait)

        x = x_ref[pl.ds(begin, lanes), :]
        places = [order[g * WIDE + j] for j in range(width)]
        wanted = jnp.concatenate([t_ref[jnp.minimum(p, spare - 1)] for p in places], axis=1)
        wanted = wanted - start - step * tile - lax.broadcasted_iota(jnp.int32, (8, lanes), 0)
        top, total, moment, picked = (state[g, i, :, 0:lanes] for i in range(4))
        for s in range(0, tile, sub):
            logits = lax.dot_general(
                e_ref[s : s + sub, :], x, (((1,), (1,)), ((), ())), preferred_element_type=jnp.float32
            )
            logits = logits.reshape(sub // 8, 8, lanes) * LOG2E
            index = lax.broadcasted_iota(jnp.int32, (sub // 8, 8, lanes), 0) * 8 + s
            new = jnp.maximum(top, jnp.max(logits, axis=0))
            lower = top - new
            factor = jnp.exp2(lower)
            delta = logits - new[None]
            weights = jnp.exp2(delta)
            moment = factor * (moment + total * lower) + jnp.sum(weights * delta, axis=0)
            total = factor * total + jnp.sum(weights, axis=0)
            picked = picked + jnp.sum(jnp.where(wanted[None] == index, logits, 0.0), axis=0)
            top = new
        for i, value in enumerate((top, total, moment, picked)):
            state[g, i, :, 0:lanes] = value

        @pl.when(step == steps - 1)
        def _():
            highest = jnp.max(top, axis=0, keepdims=True)
            lower = top - highest
            factor = jnp.exp2(lower)
            result = jnp.concatenate(
                [
                    highest,
                    jnp.sum(total * factor, axis=0, keepdims=True),
                    jnp.sum((moment + total * lower) * factor, axis=0, keepdims=True),
                    jnp.sum(picked, axis=0, keepdims=True),
                ],
                axis=0,
            )
            for j, p in enumerate(places):
                o_ref[p, 0:4] = result[:, j * BLOCK : (j + 1) * BLOCK]

    whole = (used + WIDE // 2 - 1) // WIDE

    def wide(g, carry):
        group(g, WIDE)
        return carry

    lax.fori_loop(0, whole, wide, 0)
    pl.when(whole * WIDE < used)(lambda: group(whole, WIDE // 2))


def score(call, pieces, sources, arrivals, shares, per, table, targets, lengths, stats):
    vocab, width = table.shape
    column = targets.shape[0]
    blocks = per * sum(arrival <= call for arrival in arrivals)
    capacity = -(-min(blocks, column) // WIDE) * WIDE
    tile = math.gcd(vocab, 768)
    sub = math.gcd(tile, 256)
    hbm = lambda a: pltpu.with_memory_space_constraint(a, pltpu.HBM)
    whole = lambda *shape: pl.BlockSpec(shape, lambda i, *_: (0, 0, 0))
    out = jax.ShapeDtypeStruct((column + 1, 8, BLOCK), jnp.float32)
    earlier = [] if call == 0 else [stats]
    return pl.pallas_call(
        functools.partial(score_kernel, call, sources, arrivals, shares, per, capacity, sub),
        out_shape=out,
        grid_spec=pltpu.PrefetchScalarGridSpec(
            num_scalar_prefetch=1,
            grid=(vocab // tile,),
            in_specs=[pl.BlockSpec(memory_space=pl.ANY)] * len(pieces)
            + [whole(*targets.shape), pl.BlockSpec((tile, width), lambda i, *_: (i, 0))]
            + [whole(*out.shape)] * len(earlier),
            out_specs=whole(*out.shape),
            scratch_shapes=[
                pltpu.VMEM((capacity * BLOCK, width), jnp.bfloat16),
                pltpu.VMEM((capacity // WIDE, 4, 8, WIDE * BLOCK), jnp.float32),
                pltpu.SMEM((capacity + WIDE + 1,), jnp.int32),
                pltpu.SemaphoreType.DMA((capacity,)),
            ],
        ),
        compiler_params=pltpu.CompilerParams(vmem_limit_bytes=40 * 2**20),
        cost_estimate=pl.CostEstimate(flops=2**20, bytes_accessed=2**10, transcendentals=0),
    )(lengths, *map(hbm, pieces), targets, hbm(table), *earlier)


def after(value, other):
    return lax.optimization_barrier((value, other))[0]


def finish(incoming):
    top = jnp.max(incoming[:, 0], axis=0)
    lower = incoming[:, 0] - top[None]
    factor = jnp.exp2(lower)
    total = jnp.sum(incoming[:, 1] * factor, axis=0)
    moment = jnp.sum((incoming[:, 2] + incoming[:, 1] * lower) * factor, axis=0)
    picked = jnp.sum(incoming[:, 3], axis=0)
    log_total = jnp.log(total)
    return (picked - top) * LN2 - log_total, log_total - moment * LN2 / total


def masked(results, lengths, sequence, first):
    length = lax.dynamic_slice_in_dim(lengths, sequence, 1)[0]
    valid = jnp.arange(results[0].shape[0], dtype=jnp.int32) + first < length
    return tuple(jnp.where(valid, result, 0.0) for result in results)


def column_stats(normed, table, targets, lengths):
    rows, n_tensor = normed.shape[0], lax.axis_size("tensor")
    column = rows * n_tensor // BLOCK
    targets = targets.reshape(column, 1, BLOCK)
    if 2 * rows != SLOT or n_tensor != 8:
        gathered = lax.all_gather(normed, "tensor", axis=0, tiled=True)
        return score(0, [gathered], None, [0], [], column, table, targets, lengths, None)[:column, :4]

    chips = n_tensor // 2
    swap = [(t, t ^ 1) for t in range(n_tensor)]
    along = [(2 * c, 2 * c + 2) for c in range(chips - 1)] + [(2 * c + 3, 2 * c + 1) for c in range(chips - 1)]
    along += [(n_tensor - 2, n_tensor - 1), (1, 0)]
    stages = [
        ([], [(1, 0), (1, 1)]),
        ([(1, 0), (1, 1)], [(2, 0), (2, 1)]),
        ([(2, 0), (2, 1)], [(3, 0), (3, 1)]),
        ([(3, 0)], []),
        ([(3, 1)], []),
    ]
    sources, arrivals = [(0, False), (0, True)], [0, 0]
    for stage, (arriving, _) in enumerate(stages):
        for hop, half in arriving:
            sources += [(hop, half == 1), (-hop, half == 0)]
            arrivals += [stage, stage]
    shares = [8, 16, 24, 28]

    moving = [normed, lax.ppermute(normed, "tensor", swap)]
    pieces, stats = list(moving), None
    for stage, (arriving, leaving) in enumerate(stages):
        for hop, half in arriving:
            moving[half] = after(moving[half], stats)
            pieces += [moving[half], lax.ppermute(moving[half], "tensor", swap)]
        for hop, half in leaving:
            moving[half] = lax.ppermute(moving[half], "tensor", along)
        stats = score(stage, pieces, sources, arrivals, shares, rows // BLOCK, table, targets, lengths, stats)
    return stats[:column, :4]


def shards(hidden, gain, bias, embedding, targets, lengths, owner):
    rows = hidden.shape[0]
    n_dp, n_tensor = lax.axis_size("dp"), lax.axis_size("tensor")
    tp_index, dp_index = lax.axis_index("tensor"), lax.axis_index("dp")
    group = lengths.shape[0] // n_dp
    stats = column_stats(layer_norm(hidden, gain, bias), embedding, targets, lengths)
    parts = SLOT // rows
    stats = stats.reshape(group, SLOT // BLOCK, 4, BLOCK).transpose(0, 2, 1, 3).reshape(group, 4, parts, rows)
    stats = stats.transpose(0, 2, 1, 3)
    came_from = jnp.argsort(owner).astype(jnp.int32)
    local = came_from.reshape(n_dp, group) - dp_index * group
    outgoing = jnp.zeros((n_dp, group, parts, 4, rows), jnp.float32)
    for s in range(group):
        outgoing = jnp.where((local == s)[:, :, None, None, None], stats[s][None, None], outgoing)
    incoming = lax.all_to_all(
        outgoing.reshape(n_dp * n_tensor, 4, rows), ("dp", "tensor"), split_axis=0, concat_axis=0, tiled=True
    )
    incoming = jnp.sum(incoming.reshape(n_dp, n_tensor, 4, rows), axis=0)
    sequence = lax.dynamic_slice_in_dim(came_from, dp_index * group + tp_index // parts, 1)[0]
    return masked(finish(incoming), lengths, sequence, tp_index % parts * rows)


def solution(mesh):
    in_specs = (P(("dp", "tensor"), None), P(), P(), P("tensor", None), P("dp"), P(), P())
    out_specs = (P(("dp", "tensor")), P(("dp", "tensor")))
    return jax.shard_map(shards, mesh=mesh, in_specs=in_specs, out_specs=out_specs, check_vma=False)
```

time: 392 us -> 225 us (0.57)
  Pallas kernels: 0 us -> 135 us
  matrix products: 115 us -> 0 us
  waiting for transfers between devices: 150 us -> 38.1 us
  blocking collectives: 60.7 us -> 0 us
  other arithmetic: 48.4 us -> 7.21 us
  starting transfers between devices: 0.04 us -> 33.5 us
  between operations: 14.1 us -> 2.92 us
  local copies, waits for them, and re-layouts: 3.12 us -> 9.07 us
    all_gather x1 -> x0, waiting for transfers between devices: 150 us -> none  [shards(): lax.all_gather(layer_norm(hidden, gain, bias), 'tensor', axis=0, tiled=True)]
    pallas_call x0 -> x5, Pallas kernels: none -> 135 us  [score(): pl.pallas_call(functools.partial(score_kernel, call, sources, arrivals, s...]
    dot_general x2 -> x0, matrix products: 115 us -> none  [the longest x1 115 us: shards(): lax.dot_general(lax.all_gather(layer_norm(hidden, gain, bias), 'tensor',...]
    reduce_sum x2, other arithmetic: 38.4 us -> 0.08 us  [the longest x1 0.05 us: shards(): incoming = jnp.sum(incoming.reshape(n_dp, n_tensor, 4, rows), axis=0)]
    ppermute x0 -> x13, waiting for transfers between devices: none -> 30.9 us  [the longest x6 22.7 us: column_stats(): moving[half] = lax.ppermute(moving[half], 'tensor', along)]
    psum x1 -> x0, blocking collectives: 26.4 us -> none  [shards(): lax.psum((gathered[1] * factor, gathered[2] * factor, gathered[3]), 'tens...]
    pmax x1 -> x0, blocking collectives: 26 us -> none  [shards(): top = lax.pmax(local_top, 'tensor')]
    all_to_all x0 -> x1, starting transfers between devices: none -> 18 us  [shards(): lax.all_to_all(outgoing.reshape(n_dp * n_tensor, 4, rows), ('dp', 'tensor...]
  transfers between devices with their start and end apart: 1 -> 14, of which waited for: 1 -> 9; matrix products, arithmetic and copies ran while one was open for 1% -> 2% of each run, Pallas kernels for 0% -> 50%
where the time goes in v2:
time: 225 us
  Pallas kernels  135 us (60%)
  waiting for transfers between devices  38.1 us (17%)
  starting transfers between devices  33.5 us (15%)
  local copies, waits for them, and re-layouts  9.07 us (4%)
  other arithmetic  7.21 us (3%)
  between operations  2.92 us (1%)
    pallas_call x5, Pallas kernels, score(): pl.pallas_call(functools.partial(score_kernel, call, sources, arrivals, s...  135 us
    ppermute x6, waiting for transfers between devices, column_stats(): moving[half] = lax.ppermute(moving[half], 'tensor', along)  22.7 us
    all_to_all x1, starting transfers between devices, shards(): lax.all_to_all(outgoing.reshape(n_dp * n_tensor, 4, rows), ('dp', 'tensor...  18 us
    ppermute x6, starting transfers between devices, column_stats(): moving[half] = lax.ppermute(moving[half], 'tensor', along)  14.4 us
    all_to_all x1, waiting for transfers between devices, shards(): lax.all_to_all(outgoing.reshape(n_dp * n_tensor, 4, rows), ('dp', 'tensor...  7.18 us
    ppermute x6, waiting for transfers between devices, column_stats(): pieces += [moving[half], lax.ppermute(moving[half], 'tensor', swap)]  6.97 us
    unnamed x38, local copies, waits for them, and re-layouts  6.68 us
  transfers between devices with their start and end apart: 14, of which 9 were waited for; matrix products, arithmetic and copies ran while one was open for 2% of the time, Pallas kernels for 50%

profile of v2, /device:TPU:0, one launch (start us, length us, event | category | flops | bytes accessed | tf_op | source)
XLA Modules:
  0.0 225.4 jit_solution(657888457867854126)
XLA Ops:
  0.7 2.1 convert_reduce_fusion
  5.0 2.6 %collective-permute-start.1 = (bf16[512,2048]{1,0:T(8,128)(2,1)S(1)}, bf16[512,2048]{1,0:T(8,128)(2,1)S(1)}, u32[]{:S(2)}, u32[]{:S(2)}) collective-permute-start(bf16[512,2048]{1,0:T(8,128)(2,1)S(1)} %fusion.5.refs_0_), channel_id=1, source_target_pairs={{0,2},{2,4},{4,6},{3,1},{5,3},{7,5},{6,7},{1,0},{8,10},{10,12},{12... | collective-permute-start | bytes 6291464 | tf_op jit(solution)/shard_map/ppermute | solution.py:235
  8.8 2.9 %collective-permute-start.3 = (bf16[512,2048]{1,0:T(8,128)(2,1)S(1)}, bf16[512,2048]{1,0:T(8,128)(2,1)S(1)}, u32[]{:S(2)}, u32[]{:S(2)}) collective-permute-start(bf16[512,2048]{1,0:T(8,128)(2,1)S(1)} %collective-permute-done.refs_1_), channel_id=1, source_target_pairs={{0,2},{2,4},{4,6},{3,1},{5,3},{7,5},{6,7},{1,0},{8,10},{10,12},{12... | collective-permute-start | bytes 6291464 | tf_op jit(solution)/shard_map/ppermute | solution.py:235
  11.7 31.7 %shard_map.86.refs_8_ = f32[33,8,128]{2,1,0:T(8,128)S(1)} custom-call(s32[16]{0:T(128)S(1)} %copy-done.1, bf16[512,2048]{1,0:T(8,128)(2,1)} %copy-done.2, bf16[512,2048]{1,0:T(8,128)(2,1)} %copy-done.3, s32[32,1,128]{2,1,0:T(1,128)S(1)} %bitcast.55, bf16[6144,2048]{1,0:T(8,128)(2,1)} %refs_15_.1), custom_call_target="tpu_custom_call" | custom-call | flops 1048576 | bytes 1024 | tf_op jit(solution)/shard_map/pallas_call | solution.py:159
  43.5 10.0 %collective-permute-done.3.refs_4_ = bf16[512,2048]{1,0:T(8,128)(2,1)S(1)} collective-permute-done((bf16[512,2048]{1,0:T(8,128)(2,1)S(1)}, bf16[512,2048]{1,0:T(8,128)(2,1)S(1)}, u32[]{:S(2)}, u32[]{:S(2)}) %collective-permute-start.3) | collective-permute-done | bytes 2097184 | tf_op jit(solution)/shard_map/ppermute | solution.py:235
  53.7 2.4 %collective-permute-start.7 = (bf16[512,2048]{1,0:T(8,128)(2,1)S(1)}, bf16[512,2048]{1,0:T(8,128)(2,1)S(1)}, u32[]{:S(2)}, u32[]{:S(2)}) collective-permute-start(bf16[512,2048]{1,0:T(8,128)(2,1)S(1)} %collective-permute-done.3.refs_4_), channel_id=1, source_target_pairs={{0,2},{2,4},{4,6},{3,1},{5,3},{7,5},{6,7},{1,0},{8,10},{10,12},{12... | collective-permute-start | bytes 6291464 | tf_op jit(solution)/shard_map/ppermute | solution.py:235
  56.1 1.6 collective-permute-start.5
  59.0 1.3 copy-done.7
  60.3 31.9 %shard_map.87.refs_12_ = f32[33,8,128]{2,1,0:T(8,128)S(1)} custom-call(s32[16]{0:T(128)S(1)} %copy-done.1, bf16[512,2048]{1,0:T(8,128)(2,1)} %copy-done.2, bf16[512,2048]{1,0:T(8,128)(2,1)} %copy-done.3, bf16[512,2048]{1,0:T(8,128)(2,1)} %copy-done.4, bf16[512,2048]{1,0:T(8,128)(2,1)} %copy-done.6, bf16[512,2048]{1,0:T(8,128)(2,1)} %copy-done.5, ...), custom_call_target="tpu_custom_call" | custom-call | flops 1048576 | bytes 1024 | tf_op jit(solution)/shard_map/pallas_call | solution.py:159
  92.4 9.7 %collective-permute-done.5.refs_6_ = bf16[512,2048]{1,0:T(8,128)(2,1)S(1)} collective-permute-done((bf16[512,2048]{1,0:T(8,128)(2,1)S(1)}, bf16[512,2048]{1,0:T(8,128)(2,1)S(1)}, u32[]{:S(2)}, u32[]{:S(2)}) %collective-permute-start.5) | collective-permute-done | bytes 2097184 | tf_op jit(solution)/shard_map/ppermute | solution.py:235
  102.2 2.4 %collective-permute-start.9 = (bf16[512,2048]{1,0:T(8,128)(2,1)S(1)}, bf16[512,2048]{1,0:T(8,128)(2,1)S(1)}, u32[]{:S(2)}, u32[]{:S(2)}) collective-permute-start(bf16[512,2048]{1,0:T(8,128)(2,1)S(1)} %collective-permute-done.5.refs_6_), channel_id=1, source_target_pairs={{0,2},{2,4},{4,6},{3,1},{5,3},{7,5},{6,7},{1,0},{8,10},{10,12},{12... | collective-permute-start | bytes 6291464 | tf_op jit(solution)/shard_map/ppermute | solution.py:235
  104.6 1.7 collective-permute-done.6.refs_7_
  106.3 1.3 copy-done.12
  107.6 32.1 %shard_map.88.refs_14_ = f32[33,8,128]{2,1,0:T(8,128)S(1)} custom-call(s32[16]{0:T(128)S(1)} %copy-done.1, bf16[512,2048]{1,0:T(8,128)(2,1)} %copy-done.2, bf16[512,2048]{1,0:T(8,128)(2,1)} %copy-done.3, bf16[512,2048]{1,0:T(8,128)(2,1)} %copy-done.4, bf16[512,2048]{1,0:T(8,128)(2,1)} %copy-done.6, bf16[512,2048]{1,0:T(8,128)(2,1)} %copy-done.5, ...), custom_call_target="tpu_custom_call" | custom-call | flops 1048576 | bytes 1024 | tf_op jit(solution)/shard_map/pallas_call | solution.py:159
  139.9 2.5 %collective-permute-start.11 = (bf16[512,2048]{1,0:T(8,128)(2,1)}, bf16[512,2048]{1,0:T(8,128)(2,1)}, u32[]{:S(2)}, u32[]{:S(2)}) collective-permute-start(bf16[512,2048]{1,0:T(8,128)(2,1)} %copy-done.9), channel_id=1, source_target_pairs={{0,2},{2,4},{4,6},{3,1},{5,3},{7,5},{6,7},{1,0},{8,10},{10,12},{12... | collective-permute-start | bytes 6291464 | tf_op jit(solution)/shard_map/ppermute | solution.py:235
  142.4 3.2 %collective-permute-done.10.refs_11_ = bf16[512,2048]{1,0:T(8,128)(2,1)S(1)} collective-permute-done((bf16[512,2048]{1,0:T(8,128)(2,1)S(1)}, bf16[512,2048]{1,0:T(8,128)(2,1)S(1)}, u32[]{:S(2)}, u32[]{:S(2)}) %collective-permute-start.10) | collective-permute-done | bytes 2097184 | tf_op jit(solution)/shard_map/ppermute | solution.py:233
  145.5 1.3 copy-done.14
  146.9 16.4 %shard_map.89.refs_16_ = f32[33,8,128]{2,1,0:T(8,128)S(1)} custom-call(s32[16]{0:T(128)S(1)} %copy-done.1, bf16[512,2048]{1,0:T(8,128)(2,1)} %copy-done.2, bf16[512,2048]{1,0:T(8,128)(2,1)} %copy-done.3, bf16[512,2048]{1,0:T(8,128)(2,1)} %copy-done.4, bf16[512,2048]{1,0:T(8,128)(2,1)} %copy-done.6, bf16[512,2048]{1,0:T(8,128)(2,1)} %copy-done.5, ...), custom_call_target="tpu_custom_call" | custom-call | flops 1048576 | bytes 1024 | tf_op jit(solution)/shard_map/pallas_call | solution.py:159
  163.3 3.0 %collective-permute-done.11.refs_12_ = bf16[512,2048]{1,0:T(8,128)(2,1)} collective-permute-done((bf16[512,2048]{1,0:T(8,128)(2,1)}, bf16[512,2048]{1,0:T(8,128)(2,1)}, u32[]{:S(2)}, u32[]{:S(2)}) %collective-permute-start.11) | collective-permute-done | bytes 2097184 | tf_op jit(solution)/shard_map/ppermute | solution.py:235
  168.6 2.0 collective-permute-done.12.refs_13_
  170.6 1.3 copy-done.15
  171.9 22.6 %shard_map.90 = f32[33,8,128]{2,1,0:T(8,128)S(1)} custom-call(s32[16]{0:T(128)S(1)} %copy-done.1, bf16[512,2048]{1,0:T(8,128)(2,1)} %copy-done.2, bf16[512,2048]{1,0:T(8,128)(2,1)} %copy-done.3, bf16[512,2048]{1,0:T(8,128)(2,1)} %copy-done.4, bf16[512,2048]{1,0:T(8,128)(2,1)} %copy-done.6, bf16[512,2048]{1,0:T(8,128)(2,1)} %copy-done.5, ...), custom_call_target="tpu_custom_call" | custom-call | flops 1048576 | bytes 1024 | tf_op jit(solution)/shard_map/pallas_call | solution.py:159
  195.6 18.0 %all-to-all-start = ((f32[32,4,512]{2,1,0:T(4,128)}), f32[32,4,512]{2,1,0:T(4,128)S(1)}, u32[]{:S(2)}, u32[]{:S(2)}) async-start(f32[32,4,512]{2,1,0:T(4,128)} %fusion.8), calls=%async_computation | async-start | bytes 524288 | tf_op jit(solution)/shard_map/all_to_all | solution.py:254
  216.8 7.2 %all-to-all-done = f32[32,4,512]{2,1,0:T(4,128)S(1)} async-done(((f32[32,4,512]{2,1,0:T(4,128)}), f32[32,4,512]{2,1,0:T(4,128)S(1)}, u32[]{:S(2)}, u32[]{:S(2)}) %all-to-all-start) | async-done | bytes 262176 | tf_op jit(solution)/shard_map/all_to_all | solution.py:254
  (83 shorter events, 11.2 us)
Async XLA Ops:
  3.6 8.1 %copy-start = (s32[4096]{0:T(1024)S(1)}, s32[4096]{0:T(1024)}, u32[]{:S(2)}) copy-start(s32[4096]{0:T(1024)} %param.11) | copy-start | bytes 49156
  3.6 8.1 %copy-start.1 = (s32[16]{0:T(128)S(1)}, s32[16]{0:T(128)}, u32[]{:S(2)}) copy-start(s32[16]{0:T(128)} %lengths_ref.9) | copy-start | bytes 196
  4.4 7.3 %copy-start.2 = (bf16[512,2048]{1,0:T(8,128)(2,1)}, bf16[512,2048]{1,0:T(8,128)(2,1)S(1)}, u32[]{:S(2)}) copy-start(bf16[512,2048]{1,0:T(8,128)(2,1)S(1)} %fusion.5.refs_0_) | copy-start | bytes 6291460
  4.4 4.3 %collective-permute-start = (bf16[512,2048]{1,0:T(8,128)(2,1)S(1)}, bf16[512,2048]{1,0:T(8,128)(2,1)S(1)}, u32[]{:S(2)}, u32[]{:S(2)}) collective-permute-start(bf16[512,2048]{1,0:T(8,128)(2,1)S(1)} %fusion.5.refs_0_), channel_id=1, source_target_pairs={{0,1},{1,0},{2,3},{3,2},{4,5},{5,4},{6,7},{7,6},{8,9},{9,8},{10,11... | collective-permute-start | bytes 6291464 | tf_op jit(solution)/shard_map/ppermute | solution.py:228
  5.0 38.5 %collective-permute-start.1 = (bf16[512,2048]{1,0:T(8,128)(2,1)S(1)}, bf16[512,2048]{1,0:T(8,128)(2,1)S(1)}, u32[]{:S(2)}, u32[]{:S(2)}) collective-permute-start(bf16[512,2048]{1,0:T(8,128)(2,1)S(1)} %fusion.5.refs_0_), channel_id=1, source_target_pairs={{0,2},{2,4},{4,6},{3,1},{5,3},{7,5},{6,7},{1,0},{8,10},{10,12},{12... | collective-permute-start | bytes 6291464 | tf_op jit(solution)/shard_map/ppermute | solution.py:235
  8.8 3.0 %copy-start.3 = (bf16[512,2048]{1,0:T(8,128)(2,1)}, bf16[512,2048]{1,0:T(8,128)(2,1)S(1)}, u32[]{:S(2)}) copy-start(bf16[512,2048]{1,0:T(8,128)(2,1)S(1)} %collective-permute-done.refs_1_) | copy-start | bytes 6291460
  8.8 44.8 %collective-permute-start.3 = (bf16[512,2048]{1,0:T(8,128)(2,1)S(1)}, bf16[512,2048]{1,0:T(8,128)(2,1)S(1)}, u32[]{:S(2)}, u32[]{:S(2)}) collective-permute-start(bf16[512,2048]{1,0:T(8,128)(2,1)S(1)} %collective-permute-done.refs_1_), channel_id=1, source_target_pairs={{0,2},{2,4},{4,6},{3,1},{5,3},{7,5},{6,7},{1,0},{8,10},{10,12},{12... | collective-permute-start | bytes 6291464 | tf_op jit(solution)/shard_map/ppermute | solution.py:235
  43.5 14.3 %copy-start.4 = (bf16[512,2048]{1,0:T(8,128)(2,1)}, bf16[512,2048]{1,0:T(8,128)(2,1)S(1)}, u32[]{:S(2)}) copy-start(bf16[512,2048]{1,0:T(8,128)(2,1)S(1)} %collective-permute-done.1.refs_2_) | copy-start | bytes 6291460
  43.5 14.2 %collective-permute-start.2 = (bf16[512,2048]{1,0:T(8,128)(2,1)S(1)}, bf16[512,2048]{1,0:T(8,128)(2,1)S(1)}, u32[]{:S(2)}, u32[]{:S(2)}) collective-permute-start(bf16[512,2048]{1,0:T(8,128)(2,1)S(1)} %collective-permute-done.1.refs_2_), channel_id=1, source_target_pairs={{0,1},{1,0},{2,3},{3,2},{4,5},{5,4},{6,7},{7,6},{8,9},{9,8},{10,11... | collective-permute-start | bytes 6291464 | tf_op jit(solution)/shard_map/ppermute | solution.py:233
  53.6 4.2 %copy-start.5 = (bf16[512,2048]{1,0:T(8,128)(2,1)}, bf16[512,2048]{1,0:T(8,128)(2,1)S(1)}, u32[]{:S(2)}) copy-start(bf16[512,2048]{1,0:T(8,128)(2,1)S(1)} %collective-permute-done.3.refs_4_) | copy-start | bytes 6291460
  53.6 4.2 %collective-permute-start.4 = (bf16[512,2048]{1,0:T(8,128)(2,1)S(1)}, bf16[512,2048]{1,0:T(8,128)(2,1)S(1)}, u32[]{:S(2)}, u32[]{:S(2)}) collective-permute-start(bf16[512,2048]{1,0:T(8,128)(2,1)S(1)} %collective-permute-done.3.refs_4_), channel_id=1, source_target_pairs={{0,1},{1,0},{2,3},{3,2},{4,5},{5,4},{6,7},{7,6},{8,9},{9,8},{10,11... | collective-permute-start | bytes 6291464 | tf_op jit(solution)/shard_map/ppermute | solution.py:233
  53.7 38.6 %collective-permute-start.7 = (bf16[512,2048]{1,0:T(8,128)(2,1)S(1)}, bf16[512,2048]{1,0:T(8,128)(2,1)S(1)}, u32[]{:S(2)}, u32[]{:S(2)}) collective-permute-start(bf16[512,2048]{1,0:T(8,128)(2,1)S(1)} %collective-permute-done.3.refs_4_), channel_id=1, source_target_pairs={{0,2},{2,4},{4,6},{3,1},{5,3},{7,5},{6,7},{1,0},{8,10},{10,12},{12... | collective-permute-start | bytes 6291464 | tf_op jit(solution)/shard_map/ppermute | solution.py:235
  56.1 46.0 %collective-permute-start.5 = (bf16[512,2048]{1,0:T(8,128)(2,1)S(1)}, bf16[512,2048]{1,0:T(8,128)(2,1)S(1)}, u32[]{:S(2)}, u32[]{:S(2)}) collective-permute-start(bf16[512,2048]{1,0:T(8,128)(2,1)S(1)} %collective-permute-done.1.refs_2_), channel_id=1, source_target_pairs={{0,2},{2,4},{4,6},{3,1},{5,3},{7,5},{6,7},{1,0},{8,10},{10,12},{12... | collective-permute-start | bytes 6291464 | tf_op jit(solution)/shard_map/ppermute | solution.py:235
  92.3 14.0 %copy-start.9 = (bf16[512,2048]{1,0:T(8,128)(2,1)}, bf16[512,2048]{1,0:T(8,128)(2,1)S(1)}, u32[]{:S(2)}) copy-start(bf16[512,2048]{1,0:T(8,128)(2,1)S(1)} %collective-permute-done.7.refs_8_) | copy-start | bytes 6291460
  92.3 12.3 %collective-permute-start.8 = (bf16[512,2048]{1,0:T(8,128)(2,1)S(1)}, bf16[512,2048]{1,0:T(8,128)(2,1)S(1)}, u32[]{:S(2)}, u32[]{:S(2)}) collective-permute-start(bf16[512,2048]{1,0:T(8,128)(2,1)S(1)} %collective-permute-done.7.refs_8_), channel_id=1, source_target_pairs={{0,1},{1,0},{2,3},{3,2},{4,5},{5,4},{6,7},{7,6},{8,9},{9,8},{10,11... | collective-permute-start | bytes 6291464 | tf_op jit(solution)/shard_map/ppermute | solution.py:233
  102.1 4.2 %copy-start.10 = (bf16[512,2048]{1,0:T(8,128)(2,1)}, bf16[512,2048]{1,0:T(8,128)(2,1)S(1)}, u32[]{:S(2)}) copy-start(bf16[512,2048]{1,0:T(8,128)(2,1)S(1)} %collective-permute-done.5.refs_6_) | copy-start | bytes 6291460
  102.1 4.2 %collective-permute-start.6 = (bf16[512,2048]{1,0:T(8,128)(2,1)S(1)}, bf16[512,2048]{1,0:T(8,128)(2,1)S(1)}, u32[]{:S(2)}, u32[]{:S(2)}) collective-permute-start(bf16[512,2048]{1,0:T(8,128)(2,1)S(1)} %collective-permute-done.5.refs_6_), channel_id=1, source_target_pairs={{0,1},{1,0},{2,3},{3,2},{4,5},{5,4},{6,7},{7,6},{8,9},{9,8},{10,11... | collective-permute-start | bytes 6291464 | tf_op jit(solution)/shard_map/ppermute | solution.py:233
  102.2 37.5 %collective-permute-start.9 = (bf16[512,2048]{1,0:T(8,128)(2,1)S(1)}, bf16[512,2048]{1,0:T(8,128)(2,1)S(1)}, u32[]{:S(2)}, u32[]{:S(2)}) collective-permute-start(bf16[512,2048]{1,0:T(8,128)(2,1)S(1)} %collective-permute-done.5.refs_6_), channel_id=1, source_target_pairs={{0,2},{2,4},{4,6},{3,1},{5,3},{7,5},{6,7},{1,0},{8,10},{10,12},{12... | collective-permute-start | bytes 6291464 | tf_op jit(solution)/shard_map/ppermute | solution.py:235
  139.7 26.6 %copy-start.18 = (s32[16]{0:T(128)S(1)}, s32[16]{0:T(128)}, u32[]{:S(2)}) copy-start(s32[16]{0:T(128)} %param.13) | copy-start | bytes 196
  139.7 5.9 %copy-start.13 = (bf16[512,2048]{1,0:T(8,128)(2,1)}, bf16[512,2048]{1,0:T(8,128)(2,1)S(1)}, u32[]{:S(2)}) copy-start(bf16[512,2048]{1,0:T(8,128)(2,1)S(1)} %collective-permute-done.9.refs_10_) | copy-start | bytes 6291460
  139.7 5.8 %collective-permute-start.10 = (bf16[512,2048]{1,0:T(8,128)(2,1)S(1)}, bf16[512,2048]{1,0:T(8,128)(2,1)S(1)}, u32[]{:S(2)}, u32[]{:S(2)}) collective-permute-start(bf16[512,2048]{1,0:T(8,128)(2,1)S(1)} %collective-permute-done.9.refs_10_), channel_id=1, source_target_pairs={{0,1},{1,0},{2,3},{3,2},{4,5},{5,4},{6,7},{7,6},{8,9},{9,8},{10,11... | collective-permute-start | bytes 6291464 | tf_op jit(solution)/shard_map/ppermute | solution.py:233
  139.9 26.3 %collective-permute-start.11 = (bf16[512,2048]{1,0:T(8,128)(2,1)}, bf16[512,2048]{1,0:T(8,128)(2,1)}, u32[]{:S(2)}, u32[]{:S(2)}) collective-permute-start(bf16[512,2048]{1,0:T(8,128)(2,1)} %copy-done.9), channel_id=1, source_target_pairs={{0,2},{2,4},{4,6},{3,1},{5,3},{7,5},{6,7},{1,0},{8,10},{10,12},{12... | collective-permute-start | bytes 6291464 | tf_op jit(solution)/shard_map/ppermute | solution.py:235
  166.2 4.4 %collective-permute-start.12 = (bf16[512,2048]{1,0:T(8,128)(2,1)}, bf16[512,2048]{1,0:T(8,128)(2,1)S(1)}, u32[]{:S(2)}, u32[]{:S(2)}) collective-permute-start(bf16[512,2048]{1,0:T(8,128)(2,1)} %collective-permute-done.11.refs_12_), channel_id=1, source_target_pairs={{0,1},{1,0},{2,3},{3,2},{4,5},{5,4},{6,7},{7,6},{8,9},{9,8},{10,11... | collective-permute-start | bytes 6291464 | tf_op jit(solution)/shard_map/ppermute | solution.py:233
  195.6 28.4 %all-to-all-start = ((f32[32,4,512]{2,1,0:T(4,128)}), f32[32,4,512]{2,1,0:T(4,128)S(1)}, u32[]{:S(2)}, u32[]{:S(2)}) async-start(f32[32,4,512]{2,1,0:T(4,128)} %fusion.8), calls=%async_computation | async-start | bytes 524288 | tf_op jit(solution)/shard_map/all_to_all | solution.py:254
  (9 other events, 16.3 us)

commit v3 on v2

v3 whole, which is shorter than its diff:
```python
import functools
import math

import jax
import jax.numpy as jnp
from jax import lax
from jax.experimental import pallas as pl
from jax.experimental.pallas import tpu as pltpu
from jax.sharding import PartitionSpec as P

SLOT = 1024
BLOCK = 128
WIDE = 4
ROOM = 30
EPS = 1e-05
LOG2E = 1.4426950408889634
LN2 = 0.6931471805599453
LOWEST = -1e30


def layer_norm(states, gain, bias):
    values = states.astype(jnp.float32)
    center = values - jnp.mean(values, axis=-1, keepdims=True)
    spread = jnp.mean(center * center, axis=-1, keepdims=True)
    return (center * lax.rsqrt(spread + EPS) * gain + bias).astype(jnp.bfloat16)


def score_kernel(call, sources, arrivals, limit, per, tile, sub, streamed, lengths_ref, *refs):
    count = sum(arrival <= call for arrival in arrivals)
    rows_refs, (t_ref, e_ref), refs = refs[:count], refs[count : count + 2], refs[count + 2 :]
    stats_ref, (o_ref, x_ref, state, order, sems) = (None if call == 0 else refs[0]), refs[-5:]
    at_tile, tiles = (pl.program_id(0), pl.num_programs(0)) if streamed else (0, e_ref.shape[0] // tile)
    once = pl.when(at_tile == 0) if streamed else lambda f: f()
    spare = o_ref.shape[0] - 1
    slots = SLOT // BLOCK
    n_dp, n_tensor = lax.axis_size("dp"), lax.axis_size("tensor")
    before = lax.axis_index("dp") * (lengths_ref.shape[0] // n_dp)
    start = lax.axis_index("tensor") * (tiles * tile)
    chip, core = lax.axis_index("tensor") // 2, lax.axis_index("tensor") % 2

    def copy(ref, j, place):
        return pltpu.make_async_copy(
            ref.at[pl.ds(j * BLOCK, BLOCK)],
            x_ref.at[pl.ds(pl.multiple_of(place * BLOCK, BLOCK), BLOCK)],
            sems.at[place],
        )

    def first_of(i):
        if sources is None:
            return jnp.int32(0), True
        away, crossed = sources[i]
        layer = chip + away * (2 * core - 1)
        half = core if not crossed else 1 - core
        inside = (layer >= 0) & (layer < n_tensor // 2)
        return jnp.clip(layer, 0, n_tensor // 2 - 1) * slots + half * per, inside

    @once
    def _():
        taken, arrived = jnp.int32(0), jnp.int32(0)
        for earlier in range(call):
            for i in range(count):
                if arrivals[i] == earlier:
                    first, inside = first_of(i)
                    length = lengths_ref[before + first // slots] - first % slots * BLOCK
                    held = jnp.clip((length + BLOCK - 1) // BLOCK, 0, per)
                    arrived = arrived + jnp.where(inside, held, 0)
            taken = jnp.minimum(taken + limit, arrived)
        used, rank = jnp.int32(0), jnp.int32(0)
        for i in range(count):
            first, inside = first_of(i)
            for j in range(per):
                place = first + j
                live = inside & (lengths_ref[before + place // slots] > place % slots * BLOCK)
                mine = live & (rank >= taken) & (rank < taken + limit)

                @pl.when(mine)
                def _():
                    order[used] = place
                    copy(rows_refs[i], j, used).start()

                used = used + mine.astype(jnp.int32)
                rank = rank + live.astype(jnp.int32)
        for j in range(WIDE):
            order[used + j] = spare
        order[limit + WIDE] = used
        o_ref[...] = jnp.zeros_like(o_ref) if stats_ref is None else stats_ref[...]

    used = order[limit + WIDE]

    def group(g, width):
        lanes = width * BLOCK
        begin = pl.multiple_of(g * (WIDE * BLOCK), WIDE * BLOCK)

        @once
        def _():
            for j in range(width):
                pl.when(g * WIDE + j < used)(copy(rows_refs[0], 0, g * WIDE + j).wait)
            state[g, 0, :, 0:lanes] = jnp.full((8, lanes), LOWEST, jnp.float32)
            state[g, 1:4, :, 0:lanes] = jnp.zeros((3, 8, lanes), jnp.float32)

        x = x_ref[pl.ds(begin, lanes), :]
        places = [order[g * WIDE + j] for j in range(width)]
        target = jnp.concatenate([t_ref[jnp.minimum(p, spare - 1)] for p in places], axis=1)
        target = target - start - lax.broadcasted_iota(jnp.int32, (8, lanes), 0)

        def step(i, carry, base=0):
            top, total, moment, picked = carry
            wanted = target - (base + i) * tile
            for s in range(0, tile, sub):
                table = e_ref[pl.ds(pl.multiple_of(i * tile + s, sub), sub), :]
                logits = lax.dot_general(table, x, (((1,), (1,)), ((), ())), preferred_element_type=jnp.float32)
                logits = logits.reshape(sub // 8, 8, lanes) * LOG2E
                new = jnp.maximum(top, jnp.max(logits, axis=0))
                lower = top - new
                factor = jnp.exp2(lower)
                delta = logits - new[None]
                weights = jnp.exp2(delta)
                moment = factor * (moment + total * lower) + jnp.sum(weights * delta, axis=0)
                total = factor * total + jnp.sum(weights, axis=0)
                for r in range(sub // 8):
                    picked = jnp.where(wanted == s + r * 8, logits[r], picked)
                top = new
            return top, total, moment, picked

        def give(top, total, moment, picked):
            highest = jnp.max(top, axis=0, keepdims=True)
            lower = top - highest
            factor = jnp.exp2(lower)
            result = jnp.concatenate(
                [
                    highest,
                    jnp.sum(total * factor, axis=0, keepdims=True),
                    jnp.sum((moment + total * lower) * factor, axis=0, keepdims=True),
                    jnp.sum(picked, axis=0, keepdims=True),
                ],
                axis=0,
            )
            for j, p in enumerate(places):
                o_ref[p, 0:4] = result[:, j * BLOCK : (j + 1) * BLOCK]

        carry = tuple(state[g, i, :, 0:lanes] for i in range(4))
        if streamed:
            carry = step(0, carry, at_tile)
            for i, value in enumerate(carry):
                state[g, i, :, 0:lanes] = value
            pl.when(at_tile == tiles - 1)(functools.partial(give, *carry))
        else:
            give(*lax.fori_loop(0, tiles, step, carry))

    whole = (used + WIDE // 2 - 1) // WIDE

    def wide(g, carry):
        group(g, WIDE)
        return carry

    lax.fori_loop(0, whole, wide, 0)
    pl.when(whole * WIDE < used)(lambda: group(whole, WIDE // 2))


def score(call, pieces, sources, arrivals, limit, per, table, targets, lengths, stats):
    vocab, width = table.shape
    column = targets.shape[0]
    streamed = call in (0, 4)
    tile = math.gcd(vocab, 768 if streamed else 1536)
    sub = math.gcd(tile, 256)
    space = pltpu.HBM if streamed else pltpu.VMEM
    hbm = lambda a: pltpu.with_memory_space_constraint(a, pltpu.HBM)
    vmem = pl.BlockSpec(memory_space=pltpu.VMEM)
    whole = lambda a: pl.BlockSpec(a.shape, lambda i: (0, 0, 0)) if streamed else vmem
    earlier = [] if call == 0 else [stats]
    out = jax.ShapeDtypeStruct((column + 1, 8, BLOCK), jnp.float32)
    return pl.pallas_call(
        functools.partial(score_kernel, call, sources, arrivals, limit, per, tile, sub, streamed),
        out_shape=out,
        grid=(vocab // tile,) if streamed else (),
        in_specs=[pl.BlockSpec(memory_space=pltpu.SMEM)]
        + [pl.BlockSpec(memory_space=pl.ANY)] * len(pieces)
        + [whole(targets), pl.BlockSpec((tile, width), lambda i: (i, 0)) if streamed else vmem]
        + [whole(out)] * len(earlier),
        out_specs=whole(out),
        scratch_shapes=[
            pltpu.VMEM((limit * BLOCK, width), jnp.bfloat16),
            pltpu.VMEM((-(-limit // WIDE), 4, 8, WIDE * BLOCK), jnp.float32),
            pltpu.SMEM((limit + WIDE + 1,), jnp.int32),
            pltpu.SemaphoreType.DMA((limit,)),
        ],
        compiler_params=pltpu.CompilerParams(vmem_limit_bytes=ROOM * 2**20 + max(limit - 8, 0) * BLOCK * width * 2),
        cost_estimate=pl.CostEstimate(flops=2**20, bytes_accessed=2**10, transcendentals=0),
    )(lengths, *map(hbm, pieces), targets, pltpu.with_memory_space_constraint(table, space), *earlier)


def after(value, other):
    return lax.optimization_barrier((value, other))[0]


def finish(incoming):
    top = jnp.max(incoming[:, 0], axis=0)
    lower = incoming[:, 0] - top[None]
    factor = jnp.exp2(lower)
    total = jnp.sum(incoming[:, 1] * factor, axis=0)
    moment = jnp.sum((incoming[:, 2] + incoming[:, 1] * lower) * factor, axis=0)
    picked = jnp.sum(incoming[:, 3], axis=0)
    log_total = jnp.log(total)
    return (picked - top) * LN2 - log_total, log_total - moment * LN2 / total


def masked(results, lengths, sequence, first):
    length = lax.dynamic_slice_in_dim(lengths, sequence, 1)[0]
    valid = jnp.arange(results[0].shape[0], dtype=jnp.int32) + first < length
    return tuple(jnp.where(valid, result, 0.0) for result in results)


def column_stats(normed, table, targets, lengths):
    rows, n_tensor = normed.shape[0], lax.axis_size("tensor")
    column = rows * n_tensor // BLOCK
    targets = targets.reshape(column, 1, BLOCK)
    if 2 * rows != SLOT or n_tensor != 8:
        gathered = lax.all_gather(normed, "tensor", axis=0, tiled=True)
        return score(0, [gathered], None, [0], column, column, table, targets, lengths, None)[:column, :4]

    chips = n_tensor // 2
    swap = [(t, t ^ 1) for t in range(n_tensor)]
    along = [(2 * c, 2 * c + 2) for c in range(chips - 1)] + [(2 * c + 3, 2 * c + 1) for c in range(chips - 1)]
    along += [(n_tensor - 2, n_tensor - 1), (1, 0)]
    stages = [
        ([], [(1, 0), (1, 1)]),
        ([(1, 0), (1, 1)], [(2, 0), (2, 1)]),
        ([(2, 0), (2, 1)], [(3, 0), (3, 1)]),
        ([(3, 0)], []),
        ([(3, 1)], []),
    ]
    sources, arrivals = [(0, False), (0, True)], [0, 0]
    for stage, (arriving, _) in enumerate(stages):
        for hop, half in arriving:
            sources += [(hop, half == 1), (-hop, half == 0)]
            arrivals += [stage, stage]
    per = rows // BLOCK

    moving = [normed, lax.ppermute(normed, "tensor", swap)]
    pieces, stats = list(moving), None
    for stage, (arriving, leaving) in enumerate(stages):
        for hop, half in arriving:
            moving[half] = after(moving[half], stats)
            pieces += [moving[half], lax.ppermute(moving[half], "tensor", swap)]
        for hop, half in leaving:
            moving[half] = lax.ppermute(moving[half], "tensor", along)
        stats = score(stage, pieces, sources, arrivals, 2 * per, per, table, targets, lengths, stats)
    return stats[:column, :4]


def shards(hidden, gain, bias, embedding, targets, lengths, owner):
    rows = hidden.shape[0]
    n_dp, n_tensor = lax.axis_size("dp"), lax.axis_size("tensor")
    tp_index, dp_index = lax.axis_index("tensor"), lax.axis_index("dp")
    group = lengths.shape[0] // n_dp
    stats = column_stats(layer_norm(hidden, gain, bias), embedding, targets, lengths)
    parts = SLOT // rows
    stats = stats.reshape(group, SLOT // BLOCK, 4, BLOCK).transpose(0, 2, 1, 3).reshape(group, 4, parts, rows)
    stats = stats.transpose(0, 2, 1, 3)
    index = jnp.arange(owner.shape[0], dtype=jnp.int32)
    came_from = jnp.sum(jnp.where(owner[None, :] == index[:, None], index[None, :], 0), axis=1)
    local = came_from.reshape(n_dp, group) - dp_index * group
    outgoing = jnp.zeros((n_dp, group, parts, 4, rows), jnp.float32)
    for s in range(group):
        outgoing = jnp.where((local == s)[:, :, None, None, None], stats[s][None, None], outgoing)
    incoming = lax.all_to_all(
        outgoing.reshape(n_dp * n_tensor, 4, rows), ("dp", "tensor"), split_axis=0, concat_axis=0, tiled=True
    )
    incoming = jnp.sum(incoming.reshape(n_dp, n_tensor, 4, rows), axis=0)
    sequence = lax.dynamic_slice_in_dim(came_from, dp_index * group + tp_index // parts, 1)[0]
    return masked(finish(incoming), lengths, sequence, tp_index % parts * rows)


def solution(mesh):
    in_specs = (P(("dp", "tensor"), None), P(), P(), P("tensor", None), P("dp"), P(), P())
    out_specs = (P(("dp", "tensor")), P(("dp", "tensor")))
    return jax.shard_map(shards, mesh=mesh, in_specs=in_specs, out_specs=out_specs, check_vma=False)
```

time: 225 us -> 218 us (0.969); the launches traced: 225 us -> 216 us
  Pallas kernels: 135 us -> 105 us
  waiting for transfers between devices: 38.1 us -> 66 us
  starting transfers between devices: 33.5 us -> 26.3 us
    pallas_call x5, Pallas kernels: 135 us -> 105 us  [score(): pl.pallas_call(functools.partial(score_kernel, call, sources, arrivals, l...]
    ppermute x6, waiting for transfers between devices: 22.7 us -> 45.6 us  [column_stats(): moving[half] = lax.ppermute(moving[half], 'tensor', along)]
    all_to_all x1, starting transfers between devices: 18 us -> 11.6 us  [shards(): lax.all_to_all(outgoing.reshape(n_dp * n_tensor, 4, rows), ('dp', 'tensor...]
    ppermute x6, waiting for transfers between devices: 6.97 us -> 12 us  [column_stats(): pieces += [moving[half], lax.ppermute(moving[half], 'tensor', swap)]]
    ppermute x6, starting transfers between devices: 14.4 us -> 11.9 us  [column_stats(): moving[half] = lax.ppermute(moving[half], 'tensor', along)]
    unnamed x38 -> x44, local copies, waits for them, and re-layouts: 6.68 us -> 7.09 us
  transfers between devices with their start and end apart: 14 -> 14, of which waited for: 9 -> 9; matrix products, arithmetic and copies ran while one was open for 2% -> 1% of each run, Pallas kernels for 50% -> 41%
where the time goes in v3:
time: 218 us; the launch traced here: 216 us
  Pallas kernels  105 us (48%)
  waiting for transfers between devices  66 us (30%)
  starting transfers between devices  26.3 us (12%)
  local copies, waits for them, and re-layouts  9.41 us (4%)
  other arithmetic  5.95 us (3%)
  between operations  2.92 us (1%)
    pallas_call x5, Pallas kernels, score(): pl.pallas_call(functools.partial(score_kernel, call, sources, arrivals, l...  105 us
    ppermute x6, waiting for transfers between devices, column_stats(): moving[half] = lax.ppermute(moving[half], 'tensor', along)  45.6 us
    ppermute x6, waiting for transfers between devices, column_stats(): pieces += [moving[half], lax.ppermute(moving[half], 'tensor', swap)]  12 us
    ppermute x6, starting transfers between devices, column_stats(): moving[half] = lax.ppermute(moving[half], 'tensor', along)  11.9 us
    all_to_all x1, starting transfers between devices, shards(): lax.all_to_all(outgoing.reshape(n_dp * n_tensor, 4, rows), ('dp', 'tensor...  11.6 us
    all_to_all x1, waiting for transfers between devices, shards(): lax.all_to_all(outgoing.reshape(n_dp * n_tensor, 4, rows), ('dp', 'tensor...  7.25 us
    unnamed x44, local copies, waits for them, and re-layouts  7.09 us
  transfers between devices with their start and end apart: 14, of which 9 were waited for; matrix products, arithmetic and copies ran while one was open for 1% of the time, Pallas kernels for 41%

profile of v3, /device:TPU:0, one launch (start us, length us, event | category | flops | bytes accessed | tf_op | source)
XLA Modules:
  0.0 216.0 jit_solution(13770610051495329722)
XLA Ops:
  0.7 2.1 convert_reduce_fusion
  5.0 2.6 %collective-permute-start.1 = (bf16[512,2048]{1,0:T(8,128)(2,1)S(1)}, bf16[512,2048]{1,0:T(8,128)(2,1)S(1)}, u32[]{:S(2)}, u32[]{:S(2)}) collective-permute-start(bf16[512,2048]{1,0:T(8,128)(2,1)S(1)} %fusion.5.refs_0_), channel_id=1, source_target_pairs={{0,2},{2,4},{4,6},{3,1},{5,3},{7,5},{6,7},{1,0},{8,10},{10,12},{12... | collective-permute-start | bytes 6291464 | tf_op jit(solution)/shard_map/ppermute | solution.py:246
  8.8 2.9 %collective-permute-start.3 = (bf16[512,2048]{1,0:T(8,128)(2,1)S(1)}, bf16[512,2048]{1,0:T(8,128)(2,1)S(1)}, u32[]{:S(2)}, u32[]{:S(2)}) collective-permute-start(bf16[512,2048]{1,0:T(8,128)(2,1)S(1)} %collective-permute-done.refs_1_), channel_id=1, source_target_pairs={{0,2},{2,4},{4,6},{3,1},{5,3},{7,5},{6,7},{1,0},{8,10},{10,12},{12... | collective-permute-start | bytes 6291464 | tf_op jit(solution)/shard_map/ppermute | solution.py:246
  11.7 22.4 %shard_map.86.refs_8_ = f32[33,8,128]{2,1,0:T(8,128)S(1)} custom-call(s32[16]{0:T(128)S(1)} %copy-done.5, bf16[512,2048]{1,0:T(8,128)(2,1)} %copy-done.7, bf16[512,2048]{1,0:T(8,128)(2,1)} %copy-done.8, s32[32,1,128]{2,1,0:T(1,128)S(1)} %bitcast.58, bf16[6144,2048]{1,0:T(8,128)(2,1)} %refs_15_.1), custom_call_target="tpu_custom_call" | custom-call | flops 1048576 | bytes 1024 | tf_op jit(solution)/shard_map/pallas_call | solution.py:172
  34.8 18.8 %collective-permute-done.3.refs_4_ = bf16[512,2048]{1,0:T(8,128)(2,1)S(1)} collective-permute-done((bf16[512,2048]{1,0:T(8,128)(2,1)S(1)}, bf16[512,2048]{1,0:T(8,128)(2,1)S(1)}, u32[]{:S(2)}, u32[]{:S(2)}) %collective-permute-start.3) | collective-permute-done | bytes 2097184 | tf_op jit(solution)/shard_map/ppermute | solution.py:246
  53.7 2.4 %collective-permute-start.7 = (bf16[512,2048]{1,0:T(8,128)(2,1)S(1)}, bf16[512,2048]{1,0:T(8,128)(2,1)}, u32[]{:S(2)}, u32[]{:S(2)}) collective-permute-start(bf16[512,2048]{1,0:T(8,128)(2,1)S(1)} %collective-permute-done.3.refs_4_), channel_id=1, source_target_pairs={{0,2},{2,4},{4,6},{3,1},{5,3},{7,5},{6,7},{1,0},{8,10},{10,12},{12... | collective-permute-start | bytes 6291464 | tf_op jit(solution)/shard_map/ppermute | solution.py:246
  56.1 1.6 collective-permute-start.5
  57.7 2.4 %collective-permute-done.4.refs_5_ = bf16[512,2048]{1,0:T(8,128)(2,1)S(1)} collective-permute-done((bf16[512,2048]{1,0:T(8,128)(2,1)S(1)}, bf16[512,2048]{1,0:T(8,128)(2,1)S(1)}, u32[]{:S(2)}, u32[]{:S(2)}) %collective-permute-start.4) | collective-permute-done | bytes 2097184 | tf_op jit(solution)/shard_map/ppermute | solution.py:244
  61.4 28.5 %shard_map.87.refs_12_ = f32[33,8,128]{2,1,0:T(8,128)} custom-call(s32[16]{0:T(128)} %lengths_ref.9, bf16[512,2048]{1,0:T(8,128)(2,1)} %copy-done.7, bf16[512,2048]{1,0:T(8,128)(2,1)} %copy-done.8, bf16[512,2048]{1,0:T(8,128)(2,1)} %copy-done.9, bf16[512,2048]{1,0:T(8,128)(2,1)} %copy-done.11, bf16[512,2048]{1,0:T(8,128)(2,1)} %copy-done.10, ...), custom_call_target="tpu_custom_call" | custom-call | flops 1048576 | bytes 1024 | tf_op jit(solution)/shard_map/pallas_call | solution.py:172
  90.0 12.1 %collective-permute-done.5.refs_6_ = bf16[512,2048]{1,0:T(8,128)(2,1)} collective-permute-done((bf16[512,2048]{1,0:T(8,128)(2,1)S(1)}, bf16[512,2048]{1,0:T(8,128)(2,1)}, u32[]{:S(2)}, u32[]{:S(2)}) %collective-permute-start.5) | collective-permute-done | bytes 2097184 | tf_op jit(solution)/shard_map/ppermute | solution.py:246
  102.3 2.4 %collective-permute-start.9 = (bf16[512,2048]{1,0:T(8,128)(2,1)}, bf16[512,2048]{1,0:T(8,128)(2,1)S(1)}, u32[]{:S(2)}, u32[]{:S(2)}) collective-permute-start(bf16[512,2048]{1,0:T(8,128)(2,1)} %collective-permute-done.5.refs_6_), channel_id=1, source_target_pairs={{0,2},{2,4},{4,6},{3,1},{5,3},{7,5},{6,7},{1,0},{8,10},{10,12},{12... | collective-permute-start | bytes 6291464 | tf_op jit(solution)/shard_map/ppermute | solution.py:246
  104.7 1.8 collective-permute-done.6.refs_7_
  106.5 1.3 copy-done.15
  107.8 35.6 %shard_map.88.refs_14_ = f32[33,8,128]{2,1,0:T(8,128)} custom-call(s32[16]{0:T(128)} %lengths_ref.9, bf16[512,2048]{1,0:T(8,128)(2,1)} %copy-done.7, bf16[512,2048]{1,0:T(8,128)(2,1)} %copy-done.8, bf16[512,2048]{1,0:T(8,128)(2,1)} %copy-done.9, bf16[512,2048]{1,0:T(8,128)(2,1)} %copy-done.11, bf16[512,2048]{1,0:T(8,128)(2,1)} %copy-done.10, ...), custom_call_target="tpu_custom_call" | custom-call | flops 1048576 | bytes 1024 | tf_op jit(solution)/shard_map/pallas_call | solution.py:172
  143.7 5.1 %collective-permute-done.10.refs_11_ = bf16[512,2048]{1,0:T(8,128)(2,1)S(1)} collective-permute-done((bf16[512,2048]{1,0:T(8,128)(2,1)S(1)}, bf16[512,2048]{1,0:T(8,128)(2,1)S(1)}, u32[]{:S(2)}, u32[]{:S(2)}) %collective-permute-start.10) | collective-permute-done | bytes 2097184 | tf_op jit(solution)/shard_map/ppermute | solution.py:244
  148.8 1.4 copy-done.17
  150.2 2.7 %shard_map.89.refs_16_ = f32[33,8,128]{2,1,0:T(8,128)} custom-call(s32[16]{0:T(128)} %lengths_ref.9, bf16[512,2048]{1,0:T(8,128)(2,1)} %copy-done.7, bf16[512,2048]{1,0:T(8,128)(2,1)} %copy-done.8, bf16[512,2048]{1,0:T(8,128)(2,1)} %copy-done.9, bf16[512,2048]{1,0:T(8,128)(2,1)} %copy-done.11, bf16[512,2048]{1,0:T(8,128)(2,1)} %copy-done.10, ...), custom_call_target="tpu_custom_call" | custom-call | flops 1048576 | bytes 1024 | tf_op jit(solution)/shard_map/pallas_call | solution.py:172
  152.9 14.7 %collective-permute-done.11.refs_12_ = bf16[512,2048]{1,0:T(8,128)(2,1)} collective-permute-done((bf16[512,2048]{1,0:T(8,128)(2,1)}, bf16[512,2048]{1,0:T(8,128)(2,1)}, u32[]{:S(2)}, u32[]{:S(2)}) %collective-permute-start.11) | collective-permute-done | bytes 2097184 | tf_op jit(solution)/shard_map/ppermute | solution.py:246
  167.6 1.6 collective-permute-start.12
  170.5 2.8 %collective-permute-done.12.refs_13_ = bf16[512,2048]{1,0:T(8,128)(2,1)S(1)} collective-permute-done((bf16[512,2048]{1,0:T(8,128)(2,1)}, bf16[512,2048]{1,0:T(8,128)(2,1)S(1)}, u32[]{:S(2)}, u32[]{:S(2)}) %collective-permute-start.12) | collective-permute-done | bytes 2097184 | tf_op jit(solution)/shard_map/ppermute | solution.py:244
  173.3 1.3 copy-done.18
  175.5 16.1 %shard_map.90 = f32[33,8,128]{2,1,0:T(8,128)S(1)} custom-call(s32[16]{0:T(128)S(1)} %copy-done.6, bf16[512,2048]{1,0:T(8,128)(2,1)} %copy-done.7, bf16[512,2048]{1,0:T(8,128)(2,1)} %copy-done.8, bf16[512,2048]{1,0:T(8,128)(2,1)} %copy-done.9, bf16[512,2048]{1,0:T(8,128)(2,1)} %copy-done.11, bf16[512,2048]{1,0:T(8,128)(2,1)} %copy-done.10, ...), custom_call_target="tpu_custom_call" | custom-call | flops 1048576 | bytes 1024 | tf_op jit(solution)/shard_map/pallas_call | solution.py:172
  192.7 11.6 %all-to-all-start = ((f32[32,4,512]{2,1,0:T(4,128)}), f32[32,4,512]{2,1,0:T(4,128)S(1)}, u32[]{:S(2)}, u32[]{:S(2)}) async-start(f32[32,4,512]{2,1,0:T(4,128)} %fusion.8), calls=%async_computation | async-start | bytes 524288 | tf_op jit(solution)/shard_map/all_to_all | solution.py:266
  207.4 7.2 %all-to-all-done = f32[32,4,512]{2,1,0:T(4,128)S(1)} async-done(((f32[32,4,512]{2,1,0:T(4,128)}), f32[32,4,512]{2,1,0:T(4,128)S(1)}, u32[]{:S(2)}, u32[]{:S(2)}) %all-to-all-start) | async-done | bytes 262176 | tf_op jit(solution)/shard_map/all_to_all | solution.py:266
  (88 shorter events, 11.6 us)
Async XLA Ops:
  3.6 8.1 %copy-start.3 = (s32[4096]{0:T(1024)S(1)}, s32[4096]{0:T(1024)}, u32[]{:S(2)}) copy-start(s32[4096]{0:T(1024)} %param.11) | copy-start | bytes 49156
  3.6 8.1 %copy-start.5 = (s32[16]{0:T(128)S(1)}, s32[16]{0:T(128)}, u32[]{:S(2)}) copy-start(s32[16]{0:T(128)} %lengths_ref.9) | copy-start | bytes 196
  4.4 7.3 %copy-start.7 = (bf16[512,2048]{1,0:T(8,128)(2,1)}, bf16[512,2048]{1,0:T(8,128)(2,1)S(1)}, u32[]{:S(2)}) copy-start(bf16[512,2048]{1,0:T(8,128)(2,1)S(1)} %fusion.5.refs_0_) | copy-start | bytes 6291460
  4.4 4.3 %collective-permute-start = (bf16[512,2048]{1,0:T(8,128)(2,1)S(1)}, bf16[512,2048]{1,0:T(8,128)(2,1)S(1)}, u32[]{:S(2)}, u32[]{:S(2)}) collective-permute-start(bf16[512,2048]{1,0:T(8,128)(2,1)S(1)} %fusion.5.refs_0_), channel_id=1, source_target_pairs={{0,1},{1,0},{2,3},{3,2},{4,5},{5,4},{6,7},{7,6},{8,9},{9,8},{10,11... | collective-permute-start | bytes 6291464 | tf_op jit(solution)/shard_map/ppermute | solution.py:239
  5.0 29.9 %collective-permute-start.1 = (bf16[512,2048]{1,0:T(8,128)(2,1)S(1)}, bf16[512,2048]{1,0:T(8,128)(2,1)S(1)}, u32[]{:S(2)}, u32[]{:S(2)}) collective-permute-start(bf16[512,2048]{1,0:T(8,128)(2,1)S(1)} %fusion.5.refs_0_), channel_id=1, source_target_pairs={{0,2},{2,4},{4,6},{3,1},{5,3},{7,5},{6,7},{1,0},{8,10},{10,12},{12... | collective-permute-start | bytes 6291464 | tf_op jit(solution)/shard_map/ppermute | solution.py:246
  8.8 44.8 %collective-permute-start.3 = (bf16[512,2048]{1,0:T(8,128)(2,1)S(1)}, bf16[512,2048]{1,0:T(8,128)(2,1)S(1)}, u32[]{:S(2)}, u32[]{:S(2)}) collective-permute-start(bf16[512,2048]{1,0:T(8,128)(2,1)S(1)} %collective-permute-done.refs_1_), channel_id=1, source_target_pairs={{0,2},{2,4},{4,6},{3,1},{5,3},{7,5},{6,7},{1,0},{8,10},{10,12},{12... | collective-permute-start | bytes 6291464 | tf_op jit(solution)/shard_map/ppermute | solution.py:246
  11.7 49.7 %copy-start = (bf16[6144,2048]{1,0:T(8,128)(2,1)S(1)}, bf16[6144,2048]{1,0:T(8,128)(2,1)}, u32[]{:S(2)}) copy-start(bf16[6144,2048]{1,0:T(8,128)(2,1)} %refs_15_.1) | copy-start | bytes 75497472
  34.8 25.2 %copy-start.9 = (bf16[512,2048]{1,0:T(8,128)(2,1)}, bf16[512,2048]{1,0:T(8,128)(2,1)S(1)}, u32[]{:S(2)}) copy-start(bf16[512,2048]{1,0:T(8,128)(2,1)S(1)} %collective-permute-done.1.refs_2_) | copy-start | bytes 6291460
  34.8 22.8 %collective-permute-start.2 = (bf16[512,2048]{1,0:T(8,128)(2,1)S(1)}, bf16[512,2048]{1,0:T(8,128)(2,1)S(1)}, u32[]{:S(2)}, u32[]{:S(2)}) collective-permute-start(bf16[512,2048]{1,0:T(8,128)(2,1)S(1)} %collective-permute-done.1.refs_2_), channel_id=1, source_target_pairs={{0,1},{1,0},{2,3},{3,2},{4,5},{5,4},{6,7},{7,6},{8,9},{9,8},{10,11... | collective-permute-start | bytes 6291464 | tf_op jit(solution)/shard_map/ppermute | solution.py:244
  53.6 6.5 %copy-start.10 = (bf16[512,2048]{1,0:T(8,128)(2,1)}, bf16[512,2048]{1,0:T(8,128)(2,1)S(1)}, u32[]{:S(2)}) copy-start(bf16[512,2048]{1,0:T(8,128)(2,1)S(1)} %collective-permute-done.3.refs_4_) | copy-start | bytes 6291460
  53.6 6.5 %collective-permute-start.4 = (bf16[512,2048]{1,0:T(8,128)(2,1)S(1)}, bf16[512,2048]{1,0:T(8,128)(2,1)S(1)}, u32[]{:S(2)}, u32[]{:S(2)}) collective-permute-start(bf16[512,2048]{1,0:T(8,128)(2,1)S(1)} %collective-permute-done.3.refs_4_), channel_id=1, source_target_pairs={{0,1},{1,0},{2,3},{3,2},{4,5},{5,4},{6,7},{7,6},{8,9},{9,8},{10,11... | collective-permute-start | bytes 6291464 | tf_op jit(solution)/shard_map/ppermute | solution.py:244
  53.7 36.2 %collective-permute-start.7 = (bf16[512,2048]{1,0:T(8,128)(2,1)S(1)}, bf16[512,2048]{1,0:T(8,128)(2,1)}, u32[]{:S(2)}, u32[]{:S(2)}) collective-permute-start(bf16[512,2048]{1,0:T(8,128)(2,1)S(1)} %collective-permute-done.3.refs_4_), channel_id=1, source_target_pairs={{0,2},{2,4},{4,6},{3,1},{5,3},{7,5},{6,7},{1,0},{8,10},{10,12},{12... | collective-permute-start | bytes 6291464 | tf_op jit(solution)/shard_map/ppermute | solution.py:246
  56.1 46.0 %collective-permute-start.5 = (bf16[512,2048]{1,0:T(8,128)(2,1)S(1)}, bf16[512,2048]{1,0:T(8,128)(2,1)}, u32[]{:S(2)}, u32[]{:S(2)}) collective-permute-start(bf16[512,2048]{1,0:T(8,128)(2,1)S(1)} %collective-permute-done.1.refs_2_), channel_id=1, source_target_pairs={{0,2},{2,4},{4,6},{3,1},{5,3},{7,5},{6,7},{1,0},{8,10},{10,12},{12... | collective-permute-start | bytes 6291464 | tf_op jit(solution)/shard_map/ppermute | solution.py:246
  89.9 14.8 %collective-permute-start.8 = (bf16[512,2048]{1,0:T(8,128)(2,1)}, bf16[512,2048]{1,0:T(8,128)(2,1)S(1)}, u32[]{:S(2)}, u32[]{:S(2)}) collective-permute-start(bf16[512,2048]{1,0:T(8,128)(2,1)} %collective-permute-done.7.refs_8_), channel_id=1, source_target_pairs={{0,1},{1,0},{2,3},{3,2},{4,5},{5,4},{6,7},{7,6},{8,9},{9,8},{10,11... | collective-permute-start | bytes 6291464 | tf_op jit(solution)/shard_map/ppermute | solution.py:244
  102.1 4.4 %collective-permute-start.6 = (bf16[512,2048]{1,0:T(8,128)(2,1)}, bf16[512,2048]{1,0:T(8,128)(2,1)S(1)}, u32[]{:S(2)}, u32[]{:S(2)}) collective-permute-start(bf16[512,2048]{1,0:T(8,128)(2,1)} %collective-permute-done.5.refs_6_), channel_id=1, source_target_pairs={{0,1},{1,0},{2,3},{3,2},{4,5},{5,4},{6,7},{7,6},{8,9},{9,8},{10,11... | collective-permute-start | bytes 6291464 | tf_op jit(solution)/shard_map/ppermute | solution.py:244
  102.3 41.2 %collective-permute-start.9 = (bf16[512,2048]{1,0:T(8,128)(2,1)}, bf16[512,2048]{1,0:T(8,128)(2,1)S(1)}, u32[]{:S(2)}, u32[]{:S(2)}) collective-permute-start(bf16[512,2048]{1,0:T(8,128)(2,1)} %collective-permute-done.5.refs_6_), channel_id=1, source_target_pairs={{0,2},{2,4},{4,6},{3,1},{5,3},{7,5},{6,7},{1,0},{8,10},{10,12},{12... | collective-permute-start | bytes 6291464 | tf_op jit(solution)/shard_map/ppermute | solution.py:246
  143.4 25.8 %copy-start.21 = (s32[16]{0:T(128)S(1)}, s32[16]{0:T(128)}, u32[]{:S(2)}) copy-start(s32[16]{0:T(128)} %param.13) | copy-start | bytes 196
  143.4 31.2 %copy-start.4 = (s32[4096]{0:T(1024)S(1)}, s32[4096]{0:T(1024)}, u32[]{:S(2)}) copy-start(s32[4096]{0:T(1024)} %param.11) | copy-start | bytes 49156
  143.4 31.2 %copy-start.6 = (s32[16]{0:T(128)S(1)}, s32[16]{0:T(128)}, u32[]{:S(2)}) copy-start(s32[16]{0:T(128)} %lengths_ref.9) | copy-start | bytes 196
  143.5 5.3 %copy-start.16 = (bf16[512,2048]{1,0:T(8,128)(2,1)}, bf16[512,2048]{1,0:T(8,128)(2,1)S(1)}, u32[]{:S(2)}) copy-start(bf16[512,2048]{1,0:T(8,128)(2,1)S(1)} %collective-permute-done.9.refs_10_) | copy-start | bytes 6291460
  143.5 5.3 %collective-permute-start.10 = (bf16[512,2048]{1,0:T(8,128)(2,1)S(1)}, bf16[512,2048]{1,0:T(8,128)(2,1)S(1)}, u32[]{:S(2)}, u32[]{:S(2)}) collective-permute-start(bf16[512,2048]{1,0:T(8,128)(2,1)S(1)} %collective-permute-done.9.refs_10_), channel_id=1, source_target_pairs={{0,1},{1,0},{2,3},{3,2},{4,5},{5,4},{6,7},{7,6},{8,9},{9,8},{10,11... | collective-permute-start | bytes 6291464 | tf_op jit(solution)/shard_map/ppermute | solution.py:244
  143.7 23.9 %collective-permute-start.11 = (bf16[512,2048]{1,0:T(8,128)(2,1)}, bf16[512,2048]{1,0:T(8,128)(2,1)}, u32[]{:S(2)}, u32[]{:S(2)}) collective-permute-start(bf16[512,2048]{1,0:T(8,128)(2,1)} %collective-permute-done.7.refs_8_), channel_id=1, source_target_pairs={{0,2},{2,4},{4,6},{3,1},{5,3},{7,5},{6,7},{1,0},{8,10},{10,12},{12... | collective-permute-start | bytes 6291464 | tf_op jit(solution)/shard_map/ppermute | solution.py:246
  167.6 5.6 %collective-permute-start.12 = (bf16[512,2048]{1,0:T(8,128)(2,1)}, bf16[512,2048]{1,0:T(8,128)(2,1)S(1)}, u32[]{:S(2)}, u32[]{:S(2)}) collective-permute-start(bf16[512,2048]{1,0:T(8,128)(2,1)} %collective-permute-done.11.refs_12_), channel_id=1, source_target_pairs={{0,1},{1,0},{2,3},{3,2},{4,5},{5,4},{6,7},{7,6},{8,9},{9,8},{10,11... | collective-permute-start | bytes 6291464 | tf_op jit(solution)/shard_map/ppermute | solution.py:244
  192.7 22.0 %all-to-all-start = ((f32[32,4,512]{2,1,0:T(4,128)}), f32[32,4,512]{2,1,0:T(4,128)S(1)}, u32[]{:S(2)}, u32[]{:S(2)}) async-start(f32[32,4,512]{2,1,0:T(4,128)} %fusion.8), calls=%async_computation | async-start | bytes 524288 | tf_op jit(solution)/shard_map/all_to_all | solution.py:266
  (12 other events, 22.1 us)
